TPU v7x, 32 devices: a whole 2x2x4 slice. The times are simulated.
32 devices in a mesh: dp: 8 (over z, y), tensor: 4 (over x, core).
Axes of the slice: x: 2, y: 2, z: 4, core: 2. Of those that a mesh axis runs over, the one named last changes fastest.
Arguments:
- tokens: bfloat16 [4096, 4096], P('dp', 'tensor'), may hold values from -6 to 6
- grad_out: bfloat16 [4096, 4096], P('dp'), may hold values from -3 to 3
- gate_pre: bfloat16 [4096, 14336], P('dp', 'tensor'), may hold values from -9 to 9
- up_value: bfloat16 [4096, 14336], P('dp', 'tensor'), may hold values from -6 to 6
- down_weight: bfloat16 [14336, 4096], P('tensor', 'dp'), may hold values from -0.09375 to 0.09375
- in_proj: bfloat16 [128, 4096], P(None, 'tensor'), may hold values from -0.09375 to 0.09375
- out_proj: bfloat16 [128, 14336], P(None, 'tensor'), may hold values from -0.046875 to 0.046875
- test_matrix: bfloat16 [16384, 128], replicated, may hold values from -0.046875 to 0.046875
Outputs:
- factor: float32 [16384, 128], P(('dp', 'tensor'))
All inputs are finite; a program needn't handle non-finite values.
Results may differ from a plain program's by a relative error of at most 0.0065.
The roundings to bfloat16 on the way count: a program that leaves them out, or rounds other values in their place, can miss the bound.
Values may be sent and summed in bfloat16 or wider, within the bound.
No kernel may reach another device: no remote copies, remote signals or barrier semaphores. Data moves between devices by JAX's collectives and lax.ppermute only.
A program may use at most 128 MiB of HBM per device.

v0:
```python
import jax
import jax.numpy as jnp
from jax import lax
from jax.sharding import PartitionSpec as P

SEQ_LEN = 128


shift_scale = 0.1
tiny_value = 1e-06


def local(tokens, grad_out, gate_pre, up_value, down_weight, in_proj, out_proj, test_matrix):
    rows = grad_out.shape[0]
    hidden_grad = lax.dot_general(
        grad_out,
        lax.all_gather(down_weight, "dp", axis=1, tiled=True),
        (((1,), (1,)), ((), ())),
        preferred_element_type=jnp.float32,
    )
    gate_wide = gate_pre.astype(jnp.float32)
    logistic = jax.nn.sigmoid(gate_wide)
    gate_grad = (
        hidden_grad * up_value.astype(jnp.float32) * logistic * (1.0 + gate_wide * (1.0 - logistic))
    ).astype(jnp.bfloat16)
    act_part = lax.dot_general(
        tokens, in_proj, (((1,), (1,)), ((), ())), preferred_element_type=jnp.float32
    )
    out_part = lax.dot_general(
        gate_grad, out_proj, (((1,), (1,)), ((), ())), preferred_element_type=jnp.float32
    )
    act_sum, out_sum = lax.psum((act_part, out_part), "tensor")
    pdim = in_proj.shape[0]
    rank_cols = test_matrix.shape[1]
    seqs_here = rows // SEQ_LEN
    act_seq = act_sum.astype(jnp.bfloat16).reshape(seqs_here, SEQ_LEN, pdim)
    out_seq = out_sum.astype(jnp.bfloat16).reshape(seqs_here, SEQ_LEN, pdim)
    proj_grad = (
        jnp.einsum("slp,slq->spq", act_seq, out_seq, preferred_element_type=jnp.float32)
        .astype(jnp.bfloat16)
        .reshape(seqs_here, pdim * pdim)
    )
    coeff = jnp.dot(proj_grad, test_matrix, preferred_element_type=jnp.float32).astype(jnp.bfloat16)
    dp_count = lax.axis_size("dp")
    tp_count = lax.axis_size("tensor")
    tp_index = lax.axis_index("tensor")
    dp_index = lax.axis_index("dp")
    width = pdim * pdim // (dp_count * tp_count)
    picked = lax.dynamic_slice_in_dim(
        proj_grad.reshape(seqs_here, dp_count, tp_count, width), tp_index, 1, 2
    ).reshape(seqs_here, dp_count * width)
    omega_wide = test_matrix.astype(jnp.float32)
    omega_picked = lax.dynamic_slice_in_dim(
        omega_wide.reshape(dp_count, tp_count, width, rank_cols), tp_index, 1, 1
    ).reshape(dp_count * width, rank_cols)
    omega_own = lax.dynamic_slice_in_dim(omega_picked, dp_index * width, width, 0)
    sketch_part = lax.dot_general(
        picked, coeff, (((0,), (0,)), ((), ())), preferred_element_type=jnp.float32
    )
    gram = lax.dot_general(
        test_matrix, test_matrix, (((0,), (0,)), ((), ())), preferred_element_type=jnp.float32
    )
    omega_sq = jnp.trace(gram)
    summed = lax.psum(sketch_part, "dp")
    core_local = lax.dot_general(
        omega_picked, summed, (((0,), (0,)), ((), ())), precision=lax.Precision.HIGHEST
    )
    square_sum, core_sketch = lax.psum((jnp.sum(summed * summed), core_local), "tensor")
    own_rows = lax.dynamic_slice_in_dim(summed, dp_index * width, width, 0)
    shift = shift_scale * jnp.sqrt(square_sum / (omega_sq + tiny_value))
    core = core_sketch + shift * gram
    core = 0.5 * (core + core.T)
    lower = jnp.linalg.cholesky(core)
    shifted = own_rows + shift * omega_own
    factor = jax.scipy.linalg.solve_triangular(lower, shifted.T, lower=True).T
    return factor


def solution(mesh):
    in_specs = (
        P("dp", "tensor"),
        P("dp", None),
        P("dp", "tensor"),
        P("dp", "tensor"),
        P("tensor", "dp"),
        P(None, "tensor"),
        P(None, "tensor"),
        P(),
    )
    out_specs = P(("dp", "tensor"), None)
    return jax.shard_map(local, mesh=mesh, in_specs=in_specs, out_specs=out_specs, check_vma=False)
```

profile of v0, /device:TPU:0, one launch (start us, length us, event | category | flops | bytes accessed | tf_op | source)
XLA Modules:
  0.0 786.8 jit_solution(10534654501211244954)
XLA Ops:
  6.5 0.7 all-gather.2.cloned.1.call-update
  7.3 0.0 all-reduce.5.cloned.1.call-start
  7.3 0.4 copy-done
  7.8 1.4 fusion.22
  9.2 561.6 %all-gather.2.cloned.1.call-done = bf16[3584,4096]{1,0:T(8,128)(2,1)} async-done(((bf16[3584,512]{1,0:T(8,128)(2,1)}), bf16[3584,4096]{1,0:T(8,128)(2,1)}) %all-gather.2.cloned.1.call-update) | async-done | bytes 29360144 | tf_op jit(solution)/shard_map/all_gather | solution.py:17
  570.7 0.0 copy-done.2
  570.7 24.6 %fusion.23 = f32[512,128]{1,0:T(8,128)S(1)} fusion(bf16[128,3584]{1,0:T(8,128)(2,1)S(1)} %copy-done.2, bf16[512,3584]{1,0:T(8,128)(2,1)} %param.10, bf16[512,3584]{1,0:T(8,128)(2,1)} %param.11, bf16[512,4096]{1,0:T(8,128)(2,1)} %param.9, bf16[3584,4096]{1,0:T(8,128)(2,1)} %all-gather.2.cloned.1.call-done), kind=kOutput, calls=%fused_computation.38 | convolution fusion | flops 15524167680 | bytes 42074112 | tf_op jit(solution)/shard_map/dot_general | solution.py:29
  595.3 17.1 %all-reduce.8 = (bf16[512,128]{1,0:T(8,128)(2,1)S(1)}, bf16[512,128]{1,0:T(8,128)(2,1)S(1)}) all-reduce(f32[512,128]{1,0:T(8,128)S(1)} %fusion.22, f32[512,128]{1,0:T(8,128)S(1)} %fusion.23), channel_id=1, replica_groups=mesh['dp'=8,'tensor'=4] {'tensor'}, use_global_device_ids=true, to_apply=%region_0.0 | all-reduce | flops 131072 | bytes 786432 | tf_op jit(solution)/shard_map/psum | solution.py:32
  612.5 0.2 convolution_convert_fusion
  612.7 0.1 reshape_reshape.3
  612.8 0.2 dynamic-slice_reduce_fusion
  613.0 4.6 fusion.6
  617.6 0.0 all-reduce.5.cloned.1.call-update
  617.6 0.0 all-reduce.7.cloned.1.call-start
  617.7 5.4 select_reduce_fusion.1
  623.1 0.1 copy.19
  623.2 2.3 constant_dynamic-slice_fusion
  625.6 2.7 copy_convert_fusion
  628.3 90.6 %all-reduce.5.cloned.1.call-done = f32[4096,128]{1,0:T(8,128)} async-done(((f32[4096,128]{1,0:T(8,128)}), f32[4096,128]{1,0:T(8,128)}) %all-reduce.5.cloned.1.call-update) | async-done | bytes 2097168 | tf_op jit(solution)/shard_map/psum | solution.py:64
  718.8 4.5 fusion.24
  723.3 0.0 all-reduce.7.cloned.1.call-update
  723.4 1.1 multiply_reduce_fusion
  725.2 7.0 psum.38
  732.9 21.4 %all-reduce.7.cloned.1.call-done = f32[128,128]{0,1:T(8,128)} async-done(((f32[128,128]{0,1:T(8,128)}), f32[128,128]{0,1:T(8,128)}) %all-reduce.7.cloned.1.call-update) | async-done | bytes 65552 | tf_op jit(solution)/shard_map/psum | solution.py:68
  754.3 0.8 multiply_add_fusion
  755.1 0.1 copy.20
  755.3 0.1 copy.21
  755.4 11.7 %cholesky.13 = f32[128,128]{1,0:T(8,128)S(1)} custom-call(f32[128,128]{1,0:T(8,128)S(1)} %fusion.19), custom_call_target="Cholesky" | custom-call | tf_op jit(solution)/shard_map/jit(cholesky)/cholesky | solution.py:73
  767.1 0.6 compare_reduce_fusion
  767.8 0.7 fusion.17
  768.4 9.8 %custom-call.7 = f32[1,128,128]{1,2,0:T(8,128)S(1)} custom-call(f32[1,128,128]{2,1,0:T(8,128)S(1)} %fusion.17), custom_call_target="InvertDiagBlocksLowerTriangular" | custom-call | tf_op jit(solution)/shard_map/jit(_solve_triangular)/triangular_solve | solution.py:75
  778.2 2.0 fusion.7
  (9 shorter events, 0.1 us)
Async XLA Ops:
  6.5 1.2 copy-start
  6.5 564.2 %copy-start.2 = (bf16[128,3584]{1,0:T(8,128)(2,1)S(1)}, bf16[128,3584]{1,0:T(8,128)(2,1)}, u32[]{:S(2)}) copy-start(bf16[128,3584]{1,0:T(8,128)(2,1)} %param.14) | copy-start | bytes 2752516
  6.5 564.2 %all-gather.2.cloned.1.call-start = ((), (), s32[]{:S(2)}) async-start(), calls=%async_computation | async-start | bytes 33030144 | tf_op jit(solution)/shard_map/all_gather | solution.py:17
  7.3 711.6 %all-reduce.5.cloned.1.call-start = ((), (), s32[]{:S(2)}) async-start(), calls=%async_computation.1 | async-start | bytes 4194304 | tf_op jit(solution)/shard_map/psum | solution.py:64
  617.6 136.7 %all-reduce.7.cloned.1.call-start = ((), (), s32[]{:S(2)}) async-start(), calls=%async_computation.2 | async-start | bytes 131072 | tf_op jit(solution)/shard_map/psum | solution.py:68
  718.8 4.5 copy-start.1
Sparse Core Ops, SparseCore 0:
  8.9 561.7 all-gather.1
  617.8 101.0 all-reduce.4
  723.5 30.7 all-reduce.6
where the time goes:
time: 787 us
  waiting for transfers between devices  674 us (86%)
  matrix products  42.8 us (5%)
  other arithmetic  27.6 us (4%)
  blocking collectives  24.2 us (3%)
  between operations  14.6 us (2%)
    all_gather x1, waiting for transfers between devices, local(): lax.all_gather(down_weight, 'dp', axis=1, tiled=True)  562 us
    psum x1, waiting for transfers between devices, local(): summed = lax.psum(sketch_part, 'dp')  90.6 us
    dot_general x1, matrix products, local(): lax.dot_general(gate_grad, out_proj, (((1,), (1,)), ((), ())), preferred_...  24.6 us
    psum x1, waiting for transfers between devices, local(): lax.psum((jnp.sum(summed * summed), core_local), 'tensor')  21.4 us
    psum x1, blocking collectives, local(): act_sum, out_sum = lax.psum((act_part, out_part), 'tensor')  17.1 us
  transfers between devices with their start and end apart: 3, of which 3 were waited for; matrix products, arithmetic and copies ran while one was open for 2% of the time, Pallas kernels for 0%

commit v1 on v0

v1 whole, which is shorter than its diff:
```python
import math

import jax
import jax.numpy as jnp
from jax import lax
from jax.sharding import Mesh, PartitionSpec as P

SEQ_LEN = 128
LINE = 4


shift_scale = 0.1
tiny_value = 1e-06

f32 = jnp.float32
bf16 = jnp.bfloat16


def swap(value, axis):
    if isinstance(axis, str):
        return lax.ppermute(value, axis, [(0, 1), (1, 0)])
    count = 2 ** len(axis)
    return lax.ppermute(value, axis, [(i, count - 1 - i) for i in range(count)])


def pick(value, index, dim):
    half = value.shape[dim] // 2
    return lax.dynamic_slice_in_dim(value, index * half, half, dim)


def dot_t(left, right):
    return lax.dot_general(left, right, (((1,), (1,)), ((), ())), preferred_element_type=f32)


def scatter_sum(part, x_index, c_index):
    kept = lax.dynamic_index_in_dim(part, c_index, 1, False)
    given = lax.dynamic_index_in_dim(part, 1 - c_index, 1, False)
    kept = kept + swap(given, "c")
    own = lax.dynamic_index_in_dim(kept, x_index, 0, False)
    other = lax.dynamic_index_in_dim(kept, 1 - x_index, 0, False)
    return own, other


def local(tokens, grad_out, gate_pre, up_value, down_weight, in_proj, out_proj, test_matrix):
    depth = lax.axis_size("z")
    z, y, x, c = (lax.axis_index(a) for a in ("z", "y", "x", "c"))
    rows = grad_out.shape[0]
    pdim = in_proj.shape[0]
    rank_cols = test_matrix.shape[1]
    seqs_here = rows // SEQ_LEN
    middle = lax.axis_size("m")
    chunk = down_weight.shape[1] * middle
    if middle > 1:
        down_weight = lax.all_gather(down_weight, "m", axis=1, tiled=True)
        grad_out = grad_out.reshape(rows, depth, middle, 2, -1).swapaxes(2, 3).reshape(rows, -1)

    keep_weight = pick(down_weight, y, 0)
    take_weight = swap(pick(down_weight, 1 - y, 0), "y")
    quarter = grad_out.shape[1] // 4
    sent = lax.dynamic_slice_in_dim(grad_out, (x * 2 + c) * quarter, quarter, 1)
    sent = swap(sent, "y")
    sent_x = swap(sent, "x")
    sent_c, sent_xc = swap(sent, "c"), swap(sent_x, "c")
    quarters = jnp.zeros_like(grad_out)
    for value, at in ((sent, x * 2 + c), (sent_x, (1 - x) * 2 + c), (sent_c, x * 2 + 1 - c), (sent_xc, (1 - x) * 2 + 1 - c)):
        quarters = lax.dynamic_update_slice_in_dim(quarters, value, at * quarter, 1)
    grad_both = jnp.concatenate((grad_out, quarters), 0)

    def both(value):
        return jnp.concatenate((pick(value, y, 1), swap(pick(value, 1 - y, 1), "y")), 0)

    gate_wide = both(gate_pre).astype(f32)
    up_wide = both(up_value).astype(f32)
    logistic = jax.nn.sigmoid(gate_wide)
    scale = up_wide * logistic * (1.0 + gate_wide * (1.0 - logistic))

    def term(piece, source, side):
        at = jnp.clip(source, 0, depth - 1) * 2 + side
        return dot_t(lax.dynamic_slice_in_dim(grad_both, at * chunk, chunk, 1), piece)

    up_moves = [(i, i + 1) for i in range(depth - 1)]
    down_moves = [(i + 1, i) for i in range(depth - 1)]
    hidden = term(keep_weight, z, y) + term(take_weight, z, 1 - y)
    rising = [keep_weight, take_weight]
    falling = [keep_weight, take_weight]
    for step in range(1, depth):
        for n, side in ((0, y), (1, 1 - y)):
            rising[n] = lax.ppermute(rising[n], "z", up_moves)
            falling[n] = lax.ppermute(falling[n], "z", down_moves)
            if 2 * step < depth:
                hidden = hidden + term(rising[n], z - step, side) + term(falling[n], z + step, side)
            else:
                from_low = z >= step
                hidden = hidden + term(
                    jnp.where(from_low, rising[n], falling[n]), jnp.where(from_low, z - step, z + step), side
                )
    gate_grad = (hidden * scale).astype(bf16)
    out_part = dot_t(gate_grad, pick(out_proj, y, 1))

    act_part = dot_t(tokens, in_proj)
    act_own, act_other = scatter_sum(act_part.reshape(2, 2, SEQ_LEN, pdim), x, c)
    act_seq = (act_own + swap(act_other, "x")).astype(bf16)

    out_blocks = out_part.reshape(2, 2, 2, SEQ_LEN, pdim)
    kept = lax.dynamic_index_in_dim(out_blocks, c, 2, False)
    given = lax.dynamic_index_in_dim(out_blocks, 1 - c, 2, False)
    kept = kept + swap(given, "c")
    own = lax.dynamic_index_in_dim(kept, x, 1, False)
    other = lax.dynamic_index_in_dim(kept, 1 - x, 1, False)
    out_seq = (own[0] + swap(other[0], "x") + swap(own[1], "y") + swap(other[1], ("y", "x"))).astype(bf16)

    proj_own = lax.dot_general(
        act_seq, out_seq, (((0,), (0,)), ((), ())), preferred_element_type=f32
    ).astype(bf16)
    gathered = [proj_own] + [
        lax.ppermute(proj_own, "z", [(i, (i + d) % depth) for i in range(depth)]) for d in range(1, depth)
    ]
    gathered = jnp.stack(gathered)
    if middle > 1:
        gathered = lax.all_gather(gathered, "m", axis=0, tiled=True)
    gathered = jnp.concatenate((gathered, swap(gathered, "x"), swap(gathered, "y"), swap(gathered, ("y", "x"))), 0)
    gathered = jnp.concatenate((gathered, swap(gathered, "c")), 0)
    seqs = gathered.shape[0]
    proj_grad = gathered.reshape(seqs, pdim * pdim)

    own_index = lax.axis_index(("z", "m", "y", "x", "c"))
    width = pdim * pdim // (depth * middle * 8)
    gram = lax.dot_general(
        test_matrix, test_matrix, (((0,), (0,)), ((), ())), preferred_element_type=f32
    )
    omega_sq = jnp.trace(gram)
    coeff_wide = jnp.dot(proj_grad, test_matrix, preferred_element_type=f32)
    coeff = coeff_wide.astype(bf16)
    overlap = dot_t(proj_grad, proj_grad)
    coeff_up = coeff.astype(f32)
    pairs = lax.dot_general(coeff_up, coeff_up, (((1,), (1,)), ((), ())), precision=lax.Precision.HIGHEST)
    square_sum = jnp.sum(overlap * pairs)
    core_sketch = lax.dot_general(
        coeff_wide, coeff_up, (((0,), (0,)), ((), ())), precision=lax.Precision.HIGHEST
    )
    own_rows = lax.dot_general(
        lax.dynamic_slice_in_dim(proj_grad, own_index * width, width, 1), coeff,
        (((0,), (0,)), ((), ())), preferred_element_type=f32,
    )
    shift = shift_scale * jnp.sqrt(square_sum / (omega_sq + tiny_value))
    core = core_sketch + shift * gram
    core = 0.5 * (core + core.T)
    lower = jnp.linalg.cholesky(core)
    omega_own = lax.dynamic_slice_in_dim(test_matrix, own_index * width, width, 0).astype(f32)
    shifted = own_rows + shift * omega_own
    return jax.scipy.linalg.solve_triangular(lower, shifted.T, lower=True).T


def solution(mesh):
    dp, tensor = mesh.shape["dp"], mesh.shape["tensor"]
    depth = math.gcd(dp // 2, LINE)
    grid = Mesh(
        mesh.devices.reshape(depth, dp // (2 * depth), 2, tensor // 2, 2), ("z", "m", "y", "x", "c")
    )
    dps, tensors = ("z", "m", "y"), ("x", "c")
    in_specs = (
        P(dps, tensors),
        P(dps, None),
        P(dps, tensors),
        P(dps, tensors),
        P(tensors, dps),
        P(None, tensors),
        P(None, tensors),
        P(),
    )
    out_specs = P(dps + tensors, None)
    return jax.shard_map(local, mesh=grid, in_specs=in_specs, out_specs=out_specs, check_vma=False)
```

time: 787 us -> 367 us (0.47)
  waiting for transfers between devices: 674 us -> 170 us
  starting transfers between devices: 0.08 us -> 57.7 us
  matrix products: 42.8 us -> 91.4 us
  blocking collectives: 24.2 us -> 0 us
  local copies, waits for them, and re-layouts: 3.31 us -> 22.3 us
  between operations: 14.6 us -> 1.92 us
    all_gather x1 -> x0, waiting for transfers between devices: 562 us -> none  [local(): lax.all_gather(down_weight, 'dp', axis=1, tiled=True)]
    ppermute x0 -> x32, waiting for transfers between devices: none -> 170 us  [the longest x6 108 us: local(): rising[n] = lax.ppermute(rising[n], 'z', up_moves)]
    psum x2 -> x0, waiting for transfers between devices: 112 us -> none  [the longest x1 90.6 us: local(): summed = lax.psum(sketch_part, 'dp')]
    ppermute x0 -> x32, starting transfers between devices: none -> 57.7 us  [the longest x6 28.8 us: local(): rising[n] = lax.ppermute(rising[n], 'z', up_moves)]
    dot_general x5 -> x17, matrix products: 35.3 us -> 84.7 us  [the longest x12 80 us: dot_t(): lax.dot_general(left, right, (((1,), (1,)), ((), ())), preferred_element_...]
    psum x2 -> x0, blocking collectives: 24.2 us -> none  [the longest x1 17.1 us: local(): act_sum, out_sum = lax.psum((act_part, out_part), 'tensor')]
  transfers between devices with their start and end apart: 3 -> 32, of which waited for: 3 -> 18; matrix products, arithmetic and copies ran while one was open for 2% -> 27% of each run, Pallas kernels for 0% -> 0%
where the time goes in v1:
time: 367 us
  waiting for transfers between devices  170 us (46%)
  matrix products  91.4 us (25%)
  starting transfers between devices  57.7 us (16%)
  other arithmetic  22.9 us (6%)
  local copies, waits for them, and re-layouts  22.3 us (6%)
    ppermute x6, waiting for transfers between devices, local(): rising[n] = lax.ppermute(rising[n], 'z', up_moves)  108 us
    dot_general x12, matrix products, dot_t(): lax.dot_general(left, right, (((1,), (1,)), ((), ())), preferred_element_...  80 us
    ppermute x15, waiting for transfers between devices, swap(): return lax.ppermute(value, axis, [(0, 1), (1, 0)])  34.1 us
    ppermute x6, starting transfers between devices, local(): rising[n] = lax.ppermute(rising[n], 'z', up_moves)  28.8 us
    ppermute x6, waiting for transfers between devices, local(): falling[n] = lax.ppermute(falling[n], 'z', down_moves)  23.3 us
    ppermute x15, starting transfers between devices, swap(): return lax.ppermute(value, axis, [(0, 1), (1, 0)])  12.8 us
    another operation x3, other arithmetic, local(): lower = jnp.linalg.cholesky(core)  12.4 us
    another operation x2, other arithmetic, local(): return jax.scipy.linalg.solve_triangular(lower, shifted.T, lower=True).T  10.5 us
  transfers between devices with their start and end apart: 32, of which 18 were waited for; matrix products, arithmetic and copies ran while one was open for 27% of the time, Pallas kernels for 0%

profile of v1, /device:TPU:0, one launch (start us, length us, event | category | flops | bytes accessed | tf_op | source)
XLA Modules:
  0.0 366.5 jit_solution(9061259997538955704)
XLA Ops:
  2.4 3.0 collective-permute-start.2
  7.6 4.7 %collective-permute-start.7 = (bf16[1792,512]{1,0:T(8,128)(2,1)S(1)}, bf16[1792,512]{1,0:T(8,128)(2,1)}, u32[]{:S(2)}, u32[]{:S(2)}) collective-permute-start(bf16[1792,512]{1,0:T(8,128)(2,1)S(1)} %get-tuple-element.10), channel_id=1, source_target_pairs={{0,8},{8,16},{16,24},{1,9},{9,17},{17,25},{2,10},{10,18},{18,26},{... | collective-permute-start | bytes 5505032 | tf_op jit(solution)/shard_map/ppermute | solution.py:88
  12.9 16.8 %collective-permute-done.2 = bf16[512,1024]{1,0:T(8,128)(2,1)} collective-permute-done((bf16[512,1024]{1,0:T(8,128)(2,1)}, bf16[512,1024]{1,0:T(8,128)(2,1)}, u32[]{:S(2)}, u32[]{:S(2)}) %collective-permute-start.2) | collective-permute-done | bytes 1048608 | tf_op jit(solution)/shard_map/ppermute | solution.py:21
  33.0 17.1 %collective-permute-done.7 = bf16[1792,512]{1,0:T(8,128)(2,1)} collective-permute-done((bf16[1792,512]{1,0:T(8,128)(2,1)S(1)}, bf16[1792,512]{1,0:T(8,128)(2,1)}, u32[]{:S(2)}, u32[]{:S(2)}) %collective-permute-start.7) | collective-permute-done | bytes 1835040 | tf_op jit(solution)/shard_map/ppermute | solution.py:88
  50.1 5.7 %collective-permute-start.11 = (bf16[1792,512]{1,0:T(8,128)(2,1)}, bf16[1792,512]{1,0:T(8,128)(2,1)}, u32[]{:S(2)}, u32[]{:S(2)}) collective-permute-start(bf16[1792,512]{1,0:T(8,128)(2,1)} %collective-permute-done.7), channel_id=1, source_target_pairs={{0,8},{8,16},{16,24},{1,9},{9,17},{17,25},{2,10},{10,18},{18,26},{... | collective-permute-start | bytes 5505032 | tf_op jit(solution)/shard_map/ppermute | solution.py:88
  55.8 12.3 %collective-permute-done.6 = bf16[1792,512]{1,0:T(8,128)(2,1)} collective-permute-done((bf16[1792,512]{1,0:T(8,128)(2,1)S(1)}, bf16[1792,512]{1,0:T(8,128)(2,1)}, u32[]{:S(2)}, u32[]{:S(2)}) %collective-permute-start.6) | collective-permute-done | bytes 1835040 | tf_op jit(solution)/shard_map/ppermute | solution.py:21
  68.1 4.9 %collective-permute-start.9 = (bf16[1792,512]{1,0:T(8,128)(2,1)}, bf16[1792,512]{1,0:T(8,128)(2,1)}, u32[]{:S(2)}, u32[]{:S(2)}) collective-permute-start(bf16[1792,512]{1,0:T(8,128)(2,1)} %collective-permute-done.6), channel_id=1, source_target_pairs={{0,8},{8,16},{16,24},{1,9},{9,17},{17,25},{2,10},{10,18},{18,26},{... | collective-permute-start | bytes 5505032 | tf_op jit(solution)/shard_map/ppermute | solution.py:88
  75.0 3.7 %constant_dynamic-slice_fusion.3 = (bf16[512,1792]{1,0:T(8,128)(2,1)}, bf16[512,1792]{1,0:T(8,128)(2,1)S(1)}) fusion(bf16[512,3584]{1,0:T(8,128)(2,1)} %param.11, s32[]{:T(128)S(6)} %select_n.126, s32[]{:T(128)S(6)} %select_n.128), kind=kLoop, calls=%fused_computation.122 | loop fusion | bytes 7340040 | tf_op jit(solution)/shard_map/dynamic_slice | solution.py:28
  88.0 7.3 %collective-permute-done.11 = bf16[1792,512]{1,0:T(8,128)(2,1)} collective-permute-done((bf16[1792,512]{1,0:T(8,128)(2,1)}, bf16[1792,512]{1,0:T(8,128)(2,1)}, u32[]{:S(2)}, u32[]{:S(2)}) %collective-permute-start.11) | collective-permute-done | bytes 1835040 | tf_op jit(solution)/shard_map/ppermute | solution.py:88
  95.4 4.5 %collective-permute-start.15 = (bf16[1792,512]{1,0:T(8,128)(2,1)}, bf16[1792,512]{1,0:T(8,128)(2,1)S(1)}, u32[]{:S(2)}, u32[]{:S(2)}) collective-permute-start(bf16[1792,512]{1,0:T(8,128)(2,1)} %collective-permute-done.11), channel_id=1, source_target_pairs={{0,8},{8,16},{16,24},{1,9},{9,17},{17,25},{2,10},{10,18},{18,26},{... | collective-permute-start | bytes 5505032 | tf_op jit(solution)/shard_map/ppermute | solution.py:88
  99.9 34.8 %collective-permute-done.9 = bf16[1792,512]{1,0:T(8,128)(2,1)} collective-permute-done((bf16[1792,512]{1,0:T(8,128)(2,1)}, bf16[1792,512]{1,0:T(8,128)(2,1)}, u32[]{:S(2)}, u32[]{:S(2)}) %collective-permute-start.9) | collective-permute-done | bytes 1835040 | tf_op jit(solution)/shard_map/ppermute | solution.py:88
  134.7 4.5 %collective-permute-start.13 = (bf16[1792,512]{1,0:T(8,128)(2,1)}, bf16[1792,512]{1,0:T(8,128)(2,1)S(1)}, u32[]{:S(2)}, u32[]{:S(2)}) collective-permute-start(bf16[1792,512]{1,0:T(8,128)(2,1)} %collective-permute-done.9), channel_id=1, source_target_pairs={{0,8},{8,16},{16,24},{1,9},{9,17},{17,25},{2,10},{10,18},{18,26},{... | collective-permute-start | bytes 5505032 | tf_op jit(solution)/shard_map/ppermute | solution.py:88
  140.5 5.1 %fusion.34 = f32[1024,1792]{1,0:T(8,128)} fusion(bf16[1792,512]{1,0:T(8,128)(2,1)S(1)} %get-tuple-element.10, s32[]{:T(128)S(6)} %select_n.125, bf16[512,4096]{1,0:T(8,128)(2,1)S(1)} %copy-done.3, bf16[512,4096]{1,0:T(8,128)(2,1)S(1)} %constant_dynamic-update-slice_fusion.15), kind=kOutput, calls=%fused_computation.56 | convolution fusion | flops 1881145344 | bytes 17563652 | tf_op jit(solution)/shard_map/dot_general | solution.py:32
  145.6 6.5 %fusion.40 = f32[1024,1792]{1,0:T(8,128)} fusion(bf16[1792,512]{1,0:T(8,128)(2,1)} %collective-permute-done.8, s32[]{:T(128)S(6)} %select_n.130, bf16[512,4096]{1,0:T(8,128)(2,1)S(1)} %copy-done.3, bf16[512,4096]{1,0:T(8,128)(2,1)S(1)} %constant_dynamic-update-slice_fusion.15), kind=kOutput, calls=%fused_computation.59 | convolution fusion | flops 1881145344 | bytes 17563652 | tf_op jit(solution)/shard_map/dot_general | solution.py:32
  152.1 6.6 %fusion.38 = f32[1024,1792]{1,0:T(8,128)} fusion(bf16[1792,512]{1,0:T(8,128)(2,1)} %collective-permute-done.7, s32[]{:T(128)S(6)} %select_n.129, bf16[512,4096]{1,0:T(8,128)(2,1)S(1)} %copy-done.3, bf16[512,4096]{1,0:T(8,128)(2,1)S(1)} %constant_dynamic-update-slice_fusion.15), kind=kOutput, calls=%fused_computation.58 | convolution fusion | flops 1881145344 | bytes 17563652 | tf_op jit(solution)/shard_map/dot_general | solution.py:32
  158.7 6.6 %fusion.36 = f32[1024,1792]{1,0:T(8,128)} fusion(bf16[1792,512]{1,0:T(8,128)(2,1)} %collective-permute-done.6, s32[]{:T(128)S(6)} %select_n.127, bf16[512,4096]{1,0:T(8,128)(2,1)S(1)} %copy-done.3, bf16[512,4096]{1,0:T(8,128)(2,1)S(1)} %constant_dynamic-update-slice_fusion.15), kind=kOutput, calls=%fused_computation.57 | convolution fusion | flops 1881145344 | bytes 17563652 | tf_op jit(solution)/shard_map/dot_general | solution.py:32
  166.5 6.6 %fusion.44 = f32[1024,1792]{1,0:T(8,128)} fusion(bf16[1792,512]{1,0:T(8,128)(2,1)} %collective-permute-done.10, s32[]{:T(128)S(6)} %select_n.132, bf16[512,4096]{1,0:T(8,128)(2,1)S(1)} %copy-done.3, bf16[512,4096]{1,0:T(8,128)(2,1)S(1)} %constant_dynamic-update-slice_fusion.15), kind=kOutput, calls=%fused_computation.61 | convolution fusion | flops 1881145344 | bytes 17563652 | tf_op jit(solution)/shard_map/dot_general | solution.py:32
  174.5 36.4 %collective-permute-done.13 = bf16[1792,512]{1,0:T(8,128)(2,1)S(1)} collective-permute-done((bf16[1792,512]{1,0:T(8,128)(2,1)}, bf16[1792,512]{1,0:T(8,128)(2,1)S(1)}, u32[]{:S(2)}, u32[]{:S(2)}) %collective-permute-start.13) | collective-permute-done | bytes 1835040 | tf_op jit(solution)/shard_map/ppermute | solution.py:88
  210.9 4.4 %collective-permute-start.17 = (bf16[1792,512]{1,0:T(8,128)(2,1)S(1)}, bf16[1792,512]{1,0:T(8,128)(2,1)S(1)}, u32[]{:S(2)}, u32[]{:S(2)}) collective-permute-start(bf16[1792,512]{1,0:T(8,128)(2,1)S(1)} %collective-permute-done.13), channel_id=1, source_target_pairs={{0,8},{8,16},{16,24},{1,9},{9,17},{17,25},{2,10},{10,18},{18,26},{... | collective-permute-start | bytes 5505032 | tf_op jit(solution)/shard_map/ppermute | solution.py:88
  216.8 6.6 %fusion.42 = f32[1024,1792]{1,0:T(8,128)} fusion(bf16[1792,512]{1,0:T(8,128)(2,1)} %collective-permute-done.9, s32[]{:T(128)S(6)} %select_n.131, bf16[512,4096]{1,0:T(8,128)(2,1)S(1)} %copy-done.3, bf16[512,4096]{1,0:T(8,128)(2,1)S(1)} %constant_dynamic-update-slice_fusion.15), kind=kOutput, calls=%fused_computation.60 | convolution fusion | flops 1881145344 | bytes 17563652 | tf_op jit(solution)/shard_map/dot_general | solution.py:32
  223.4 5.1 %fusion.12 = f32[1024,1792]{1,0:T(8,128)} fusion(bf16[1792,512]{1,0:T(8,128)(2,1)} %collective-permute-done.11, bf16[1792,512]{1,0:T(8,128)(2,1)S(1)} %collective-permute-done.12, pred[]{:T(512)S(6)} %ge.10, s32[]{:T(128)S(6)} %select_n.134, bf16[512,4096]{1,0:T(8,128)(2,1)S(1)} %copy-done.3, bf16[512,4096]{1,0:T(8,128)(2,1)S(1)} %constant_dynamic-update-slice_fusion.15), kind=kOutput, calls=%fused_computation.34 | convolution fusion | flops 1882062848 | bytes 19398660 | tf_op jit(solution)/shard_map/dot_general | solution.py:32
  228.5 5.0 %fusion.10 = f32[1024,1792]{1,0:T(8,128)} fusion(bf16[1792,512]{1,0:T(8,128)(2,1)S(1)} %collective-permute-done.13, bf16[1792,512]{1,0:T(8,128)(2,1)S(1)} %collective-permute-done.14, pred[]{:T(512)S(6)} %ge.10, s32[]{:T(128)S(6)} %select_n.137, bf16[512,4096]{1,0:T(8,128)(2,1)S(1)} %copy-done.3, bf16[512,4096]{1,0:T(8,128)(2,1)S(1)} %constant_dynamic-update-slice_fusion.15), kind=kOutput, calls=%fused_computation.32 | convolution fusion | flops 1882062848 | bytes 19398660 | tf_op jit(solution)/shard_map/dot_general | solution.py:32
  233.5 2.6 collective-permute-done.16
  236.1 5.0 %fusion.8 = f32[1024,1792]{1,0:T(8,128)} fusion(bf16[1792,512]{1,0:T(8,128)(2,1)S(1)} %collective-permute-done.15, bf16[1792,512]{1,0:T(8,128)(2,1)S(1)} %collective-permute-done.16, pred[]{:T(512)S(6)} %ge.11, s32[]{:T(128)S(6)} %select_n.140, bf16[512,4096]{1,0:T(8,128)(2,1)S(1)} %copy-done.3, bf16[512,4096]{1,0:T(8,128)(2,1)S(1)} %constant_dynamic-update-slice_fusion.15), kind=kOutput, calls=%fused_computation.30 | convolution fusion | flops 1882062848 | bytes 19398660 | tf_op jit(solution)/shard_map/dot_general | solution.py:32
  241.2 11.2 %collective-permute-done.17 = bf16[1792,512]{1,0:T(8,128)(2,1)S(1)} collective-permute-done((bf16[1792,512]{1,0:T(8,128)(2,1)S(1)}, bf16[1792,512]{1,0:T(8,128)(2,1)S(1)}, u32[]{:S(2)}, u32[]{:S(2)}) %collective-permute-start.17) | collective-permute-done | bytes 1835040 | tf_op jit(solution)/shard_map/ppermute | solution.py:88
  252.4 20.7 %collective-permute-done.18 = bf16[1792,512]{1,0:T(8,128)(2,1)S(1)} collective-permute-done((bf16[1792,512]{1,0:T(8,128)(2,1)S(1)}, bf16[1792,512]{1,0:T(8,128)(2,1)S(1)}, u32[]{:S(2)}, u32[]{:S(2)}) %collective-permute-start.18) | collective-permute-done | bytes 1835040 | tf_op jit(solution)/shard_map/ppermute | solution.py:89
  274.4 25.1 %fusion.19 = f32[1024,128]{1,0:T(8,128)S(1)} fusion(f32[1024,1792]{1,0:T(8,128)} %fusion.8, f32[1024,1792]{1,0:T(8,128)} %fusion.10, f32[1024,1792]{1,0:T(8,128)} %fusion.12, f32[1024,1792]{1,0:T(8,128)} %fusion.44, f32[1024,1792]{1,0:T(8,128)} %fusion.42, f32[1024,1792]{1,0:T(8,128)} %fusion.40, f32[1024,1792]{1,0:T(8,128)} %fusion.38, ...), kind=kOutput, calls=%fused_computation.40 | convolution fusion | flops 2401370112 | bytes 86441992 | tf_op jit(solution)/shard_map/dot_general | solution.py:32
  310.4 2.8 collective-permute-start.27
  323.6 5.7 %select_reduce_fusion.1 = (f32[]{:T(128)}, f32[128,128]{1,0:T(8,128)S(1)}) fusion(bf16[16384,128]{1,0:T(8,128)(2,1)} %param.15), kind=kOutput, calls=%fused_computation.97 | convolution fusion | flops 536920064 | bytes 4259844 | tf_op jit(solution)/shard_map/dot_general | solution.py:128
  335.8 3.0 fusion.97
  342.6 11.7 %cholesky.13 = f32[128,128]{1,0:T(8,128)S(1)} custom-call(f32[128,128]{1,0:T(8,128)S(1)} %fusion.62), custom_call_target="Cholesky" | custom-call | tf_op jit(solution)/shard_map/jit(cholesky)/cholesky | solution.py:148
  355.7 9.8 %custom-call.7 = f32[1,128,128]{1,2,0:T(8,128)S(1)} custom-call(f32[1,128,128]{2,1,0:T(8,128)S(1)} %fusion.54), custom_call_target="InvertDiagBlocksLowerTriangular" | custom-call | tf_op jit(solution)/shard_map/jit(_solve_triangular)/triangular_solve | solution.py:151
  (119 shorter events, 58.6 us)
Async XLA Ops:
  2.4 27.3 %collective-permute-start.2 = (bf16[512,1024]{1,0:T(8,128)(2,1)}, bf16[512,1024]{1,0:T(8,128)(2,1)}, u32[]{:S(2)}, u32[]{:S(2)}) collective-permute-start(bf16[512,1024]{1,0:T(8,128)(2,1)} %constant_dynamic-slice_fusion.6), channel_id=1, source_target_pairs={{0,4},{4,0},{1,5},{5,1},{2,6},{6,2},{3,7},{7,3},{8,12},{12,8},{9,1... | collective-permute-start | bytes 3145736 | tf_op jit(solution)/shard_map/ppermute | solution.py:21
  7.6 42.5 %collective-permute-start.7 = (bf16[1792,512]{1,0:T(8,128)(2,1)S(1)}, bf16[1792,512]{1,0:T(8,128)(2,1)}, u32[]{:S(2)}, u32[]{:S(2)}) collective-permute-start(bf16[1792,512]{1,0:T(8,128)(2,1)S(1)} %get-tuple-element.10), channel_id=1, source_target_pairs={{0,8},{8,16},{16,24},{1,9},{9,17},{17,25},{2,10},{10,18},{18,26},{... | collective-permute-start | bytes 5505032 | tf_op jit(solution)/shard_map/ppermute | solution.py:88
  12.4 55.8 %collective-permute-start.6 = (bf16[1792,512]{1,0:T(8,128)(2,1)S(1)}, bf16[1792,512]{1,0:T(8,128)(2,1)}, u32[]{:S(2)}, u32[]{:S(2)}) collective-permute-start(bf16[1792,512]{1,0:T(8,128)(2,1)S(1)} %get-tuple-element.9), channel_id=1, source_target_pairs={{0,4},{4,0},{1,5},{5,1},{2,6},{6,2},{3,7},{7,3},{8,12},{12,8},{9,1... | collective-permute-start | bytes 5505032 | tf_op jit(solution)/shard_map/ppermute | solution.py:21
  29.6 43.4 %collective-permute-start.3 = (bf16[512,1024]{1,0:T(8,128)(2,1)}, bf16[512,1024]{1,0:T(8,128)(2,1)}, u32[]{:S(2)}, u32[]{:S(2)}) collective-permute-start(bf16[512,1024]{1,0:T(8,128)(2,1)} %collective-permute-done.2), channel_id=1, source_target_pairs={{0,2},{2,0},{1,3},{3,1},{4,6},{6,4},{5,7},{7,5},{8,10},{10,8},{9,1... | collective-permute-start | bytes 3145736 | tf_op jit(solution)/shard_map/ppermute | solution.py:21
  31.7 43.3 %collective-permute-start.4 = (bf16[512,1024]{1,0:T(8,128)(2,1)}, bf16[512,1024]{1,0:T(8,128)(2,1)}, u32[]{:S(2)}, u32[]{:S(2)}) collective-permute-start(bf16[512,1024]{1,0:T(8,128)(2,1)} %collective-permute-done.2), channel_id=1, source_target_pairs={{0,1},{1,0},{2,3},{3,2},{4,5},{5,4},{6,7},{7,6},{8,9},{9,8},{10,11... | collective-permute-start | bytes 3145736 | tf_op jit(solution)/shard_map/ppermute | solution.py:21
  31.7 53.3 %collective-permute-start.8 = (bf16[1792,512]{1,0:T(8,128)(2,1)S(1)}, bf16[1792,512]{1,0:T(8,128)(2,1)}, u32[]{:S(2)}, u32[]{:S(2)}) collective-permute-start(bf16[1792,512]{1,0:T(8,128)(2,1)S(1)} %get-tuple-element.10), channel_id=1, source_target_pairs={{8,0},{16,8},{24,16},{9,1},{17,9},{25,17},{10,2},{18,10},{26,18},{... | collective-permute-start | bytes 5505032 | tf_op jit(solution)/shard_map/ppermute | solution.py:89
  50.1 45.3 %collective-permute-start.11 = (bf16[1792,512]{1,0:T(8,128)(2,1)}, bf16[1792,512]{1,0:T(8,128)(2,1)}, u32[]{:S(2)}, u32[]{:S(2)}) collective-permute-start(bf16[1792,512]{1,0:T(8,128)(2,1)} %collective-permute-done.7), channel_id=1, source_target_pairs={{0,8},{8,16},{16,24},{1,9},{9,17},{17,25},{2,10},{10,18},{18,26},{... | collective-permute-start | bytes 5505032 | tf_op jit(solution)/shard_map/ppermute | solution.py:88
  68.1 66.5 %collective-permute-start.9 = (bf16[1792,512]{1,0:T(8,128)(2,1)}, bf16[1792,512]{1,0:T(8,128)(2,1)}, u32[]{:S(2)}, u32[]{:S(2)}) collective-permute-start(bf16[1792,512]{1,0:T(8,128)(2,1)} %collective-permute-done.6), channel_id=1, source_target_pairs={{0,8},{8,16},{16,24},{1,9},{9,17},{17,25},{2,10},{10,18},{18,26},{... | collective-permute-start | bytes 5505032 | tf_op jit(solution)/shard_map/ppermute | solution.py:88
  73.1 66.1 %collective-permute-start.10 = (bf16[1792,512]{1,0:T(8,128)(2,1)}, bf16[1792,512]{1,0:T(8,128)(2,1)}, u32[]{:S(2)}, u32[]{:S(2)}) collective-permute-start(bf16[1792,512]{1,0:T(8,128)(2,1)} %collective-permute-done.6), channel_id=1, source_target_pairs={{8,0},{16,8},{24,16},{9,1},{17,9},{25,17},{10,2},{18,10},{26,18},{... | collective-permute-start | bytes 5505032 | tf_op jit(solution)/shard_map/ppermute | solution.py:89
  75.0 11.7 %collective-permute-start.5 = (bf16[512,1024]{1,0:T(8,128)(2,1)}, bf16[512,1024]{1,0:T(8,128)(2,1)S(1)}, u32[]{:S(2)}, u32[]{:S(2)}) collective-permute-start(bf16[512,1024]{1,0:T(8,128)(2,1)} %collective-permute-done.3), channel_id=1, source_target_pairs={{0,1},{1,0},{2,3},{3,2},{4,5},{5,4},{6,7},{7,6},{8,9},{9,8},{10,11... | collective-permute-start | bytes 3145736 | tf_op jit(solution)/shard_map/ppermute | solution.py:21
  85.0 156.1 %collective-permute-start.19 = (bf16[512,1792]{1,0:T(8,128)(2,1)S(1)}, bf16[512,1792]{1,0:T(8,128)(2,1)S(1)}, u32[]{:S(2)}, u32[]{:S(2)}) collective-permute-start(bf16[512,1792]{1,0:T(8,128)(2,1)S(1)} %get-tuple-element.8), channel_id=1, source_target_pairs={{0,4},{4,0},{1,5},{5,1},{2,6},{6,2},{3,7},{7,3},{8,12},{12,8},{9,1... | collective-permute-start | bytes 5505032 | tf_op jit(solution)/shard_map/ppermute | solution.py:21
  86.6 78.6 %collective-permute-start.12 = (bf16[1792,512]{1,0:T(8,128)(2,1)}, bf16[1792,512]{1,0:T(8,128)(2,1)S(1)}, u32[]{:S(2)}, u32[]{:S(2)}) collective-permute-start(bf16[1792,512]{1,0:T(8,128)(2,1)} %collective-permute-done.8), channel_id=1, source_target_pairs={{8,0},{16,8},{24,16},{9,1},{17,9},{25,17},{10,2},{18,10},{26,18},{... | collective-permute-start | bytes 5505032 | tf_op jit(solution)/shard_map/ppermute | solution.py:89
  95.4 78.6 %collective-permute-start.15 = (bf16[1792,512]{1,0:T(8,128)(2,1)}, bf16[1792,512]{1,0:T(8,128)(2,1)S(1)}, u32[]{:S(2)}, u32[]{:S(2)}) collective-permute-start(bf16[1792,512]{1,0:T(8,128)(2,1)} %collective-permute-done.11), channel_id=1, source_target_pairs={{0,8},{8,16},{16,24},{1,9},{9,17},{17,25},{2,10},{10,18},{18,26},{... | collective-permute-start | bytes 5505032 | tf_op jit(solution)/shard_map/ppermute | solution.py:88
  134.7 76.3 %collective-permute-start.13 = (bf16[1792,512]{1,0:T(8,128)(2,1)}, bf16[1792,512]{1,0:T(8,128)(2,1)S(1)}, u32[]{:S(2)}, u32[]{:S(2)}) collective-permute-start(bf16[1792,512]{1,0:T(8,128)(2,1)} %collective-permute-done.9), channel_id=1, source_target_pairs={{0,8},{8,16},{16,24},{1,9},{9,17},{17,25},{2,10},{10,18},{18,26},{... | collective-permute-start | bytes 5505032 | tf_op jit(solution)/shard_map/ppermute | solution.py:88
  139.2 76.1 %collective-permute-start.14 = (bf16[1792,512]{1,0:T(8,128)(2,1)}, bf16[1792,512]{1,0:T(8,128)(2,1)S(1)}, u32[]{:S(2)}, u32[]{:S(2)}) collective-permute-start(bf16[1792,512]{1,0:T(8,128)(2,1)} %collective-permute-done.10), channel_id=1, source_target_pairs={{8,0},{16,8},{24,16},{9,1},{17,9},{25,17},{10,2},{18,10},{26,18},{... | collective-permute-start | bytes 5505032 | tf_op jit(solution)/shard_map/ppermute | solution.py:89
  165.2 70.9 %collective-permute-start.16 = (bf16[1792,512]{1,0:T(8,128)(2,1)S(1)}, bf16[1792,512]{1,0:T(8,128)(2,1)S(1)}, u32[]{:S(2)}, u32[]{:S(2)}) collective-permute-start(bf16[1792,512]{1,0:T(8,128)(2,1)S(1)} %collective-permute-done.12), channel_id=1, source_target_pairs={{8,0},{16,8},{24,16},{9,1},{17,9},{25,17},{10,2},{18,10},{26,18},{... | collective-permute-start | bytes 5505032 | tf_op jit(solution)/shard_map/ppermute | solution.py:89
  174.0 67.2 %collective-permute-start.20 = (bf16[512,1792]{1,0:T(8,128)(2,1)S(1)}, bf16[512,1792]{1,0:T(8,128)(2,1)S(1)}, u32[]{:S(2)}, u32[]{:S(2)}) collective-permute-start(bf16[512,1792]{1,0:T(8,128)(2,1)S(1)} %get-tuple-element.6), channel_id=1, source_target_pairs={{0,4},{4,0},{1,5},{5,1},{2,6},{6,2},{3,7},{7,3},{8,12},{12,8},{9,1... | collective-permute-start | bytes 5505032 | tf_op jit(solution)/shard_map/ppermute | solution.py:21
  210.9 41.4 %collective-permute-start.17 = (bf16[1792,512]{1,0:T(8,128)(2,1)S(1)}, bf16[1792,512]{1,0:T(8,128)(2,1)S(1)}, u32[]{:S(2)}, u32[]{:S(2)}) collective-permute-start(bf16[1792,512]{1,0:T(8,128)(2,1)S(1)} %collective-permute-done.13), channel_id=1, source_target_pairs={{0,8},{8,16},{16,24},{1,9},{9,17},{17,25},{2,10},{10,18},{18,26},{... | collective-permute-start | bytes 5505032 | tf_op jit(solution)/shard_map/ppermute | solution.py:88
  215.3 57.7 %collective-permute-start.18 = (bf16[1792,512]{1,0:T(8,128)(2,1)S(1)}, bf16[1792,512]{1,0:T(8,128)(2,1)S(1)}, u32[]{:S(2)}, u32[]{:S(2)}) collective-permute-start(bf16[1792,512]{1,0:T(8,128)(2,1)S(1)} %collective-permute-done.14), channel_id=1, source_target_pairs={{8,0},{16,8},{24,16},{9,1},{17,9},{25,17},{10,2},{18,10},{26,18},{... | collective-permute-start | bytes 5505032 | tf_op jit(solution)/shard_map/ppermute | solution.py:89
  236.1 63.5 %collective-permute-start = (f32[2,128,128]{2,1,0:T(8,128)S(1)}, f32[2,128,128]{2,1,0:T(8,128)S(1)}, u32[]{:S(2)}, u32[]{:S(2)}) collective-permute-start(f32[2,128,128]{2,1,0:T(8,128)S(1)} %dynamic-slice_bitcast_fusion.1), channel_id=1, source_target_pairs={{0,1},{1,0},{2,3},{3,2},{4,5},{5,4},{6,7},{7,6},{8,9},{9,8},{10,11... | collective-permute-start | bytes 393224 | tf_op jit(solution)/shard_map/ppermute | solution.py:21
  299.5 1.7 collective-permute-start.21
  299.7 5.2 %collective-permute-start.1 = (f32[128,128]{1,0:T(8,128)S(1)}, f32[128,128]{1,0:T(8,128)S(1)}, u32[]{:S(2)}, u32[]{:S(2)}) collective-permute-start(f32[128,128]{1,0:T(8,128)S(1)} %dynamic-slice_bitcast_fusion.6), channel_id=1, source_target_pairs={{0,2},{2,0},{1,3},{3,1},{4,6},{6,4},{5,7},{7,5},{8,10},{10,8},{9,1... | collective-permute-start | bytes 196616 | tf_op jit(solution)/shard_map/ppermute | solution.py:21
  301.3 5.3 %collective-permute-start.24 = (f32[128,128]{1,0:T(8,128)S(1)}, f32[128,128]{1,0:T(8,128)S(1)}, u32[]{:S(2)}, u32[]{:S(2)}) collective-permute-start(f32[128,128]{1,0:T(8,128)S(1)} %get-tuple-element.12), channel_id=1, source_target_pairs={{0,6},{2,4},{4,2},{6,0},{1,7},{3,5},{5,3},{7,1},{8,14},{10,12},{12... | collective-permute-start | bytes 196616 | tf_op jit(solution)/shard_map/ppermute | solution.py:23
  303.7 4.3 %collective-permute-start.23 = (f32[128,128]{1,0:T(8,128)S(1)}, f32[128,128]{1,0:T(8,128)S(1)}, u32[]{:S(2)}, u32[]{:S(2)}) collective-permute-start(f32[128,128]{1,0:T(8,128)S(1)} %get-tuple-element.13), channel_id=1, source_target_pairs={{0,4},{4,0},{1,5},{5,1},{2,6},{6,2},{3,7},{7,3},{8,12},{12,8},{9,1... | collective-permute-start | bytes 196616 | tf_op jit(solution)/shard_map/ppermute | solution.py:21
  304.2 4.3 %collective-permute-start.22 = (f32[128,128]{1,0:T(8,128)S(1)}, f32[128,128]{1,0:T(8,128)S(1)}, u32[]{:S(2)}, u32[]{:S(2)}) collective-permute-start(f32[128,128]{1,0:T(8,128)S(1)} %get-tuple-element.11), channel_id=1, source_target_pairs={{0,2},{2,0},{1,3},{3,1},{4,6},{6,4},{5,7},{7,5},{8,10},{10,8},{9,1... | collective-permute-start | bytes 196616 | tf_op jit(solution)/shard_map/ppermute | solution.py:21
  308.7 5.9 %collective-permute-start.25 = (bf16[128,128]{1,0:T(8,128)(2,1)S(1)}, bf16[128,128]{1,0:T(8,128)(2,1)S(1)}, u32[]{:S(2)}, u32[]{:S(2)}) collective-permute-start(bf16[128,128]{1,0:T(8,128)(2,1)S(1)} %get-tuple-element.28), channel_id=1, source_target_pairs={{0,8},{8,16},{16,24},{24,0},{1,9},{9,17},{17,25},{25,1},{2,10},{10... | collective-permute-start | bytes 98312 | tf_op jit(solution)/shard_map/ppermute | solution.py:116
  309.3 6.0 %collective-permute-start.26 = (bf16[128,128]{1,0:T(8,128)(2,1)S(1)}, bf16[128,128]{1,0:T(8,128)(2,1)S(1)}, u32[]{:S(2)}, u32[]{:S(2)}) collective-permute-start(bf16[128,128]{1,0:T(8,128)(2,1)S(1)} %get-tuple-element.28), channel_id=1, source_target_pairs={{0,16},{8,24},{16,0},{24,8},{1,17},{9,25},{17,1},{25,9},{2,18},{10... | collective-permute-start | bytes 98312 | tf_op jit(solution)/shard_map/ppermute | solution.py:116
  310.4 4.9 %collective-permute-start.27 = (bf16[128,128]{1,0:T(8,128)(2,1)S(1)}, bf16[128,128]{1,0:T(8,128)(2,1)S(1)}, u32[]{:S(2)}, u32[]{:S(2)}) collective-permute-start(bf16[128,128]{1,0:T(8,128)(2,1)S(1)} %get-tuple-element.28), channel_id=1, source_target_pairs={{0,24},{8,0},{16,8},{24,16},{1,25},{9,1},{17,9},{25,17},{2,26},{10... | collective-permute-start | bytes 98312 | tf_op jit(solution)/shard_map/ppermute | solution.py:116
  315.3 6.0 %collective-permute-start.28 = (bf16[4,128,128]{2,1,0:T(8,128)(2,1)S(1)}, bf16[4,128,128]{2,1,0:T(8,128)(2,1)S(1)}, u32[]{:S(2)}, u32[]{:S(2)}) collective-permute-start(bf16[4,128,128]{2,1,0:T(8,128)(2,1)S(1)} %pad_maximum_fusion), channel_id=1, source_target_pairs={{0,2},{2,0},{1,3},{3,1},{4,6},{6,4},{5,7},{7,5},{8,10},{10,8},{9,1... | collective-permute-start | bytes 393224 | tf_op jit(solution)/shard_map/ppermute | solution.py:21
  316.0 6.0 %collective-permute-start.29 = (bf16[4,128,128]{2,1,0:T(8,128)(2,1)S(1)}, bf16[4,128,128]{2,1,0:T(8,128)(2,1)S(1)}, u32[]{:S(2)}, u32[]{:S(2)}) collective-permute-start(bf16[4,128,128]{2,1,0:T(8,128)(2,1)S(1)} %pad_maximum_fusion), channel_id=1, source_target_pairs={{0,4},{4,0},{1,5},{5,1},{2,6},{6,2},{3,7},{7,3},{8,12},{12,8},{9,1... | collective-permute-start | bytes 393224 | tf_op jit(solution)/shard_map/ppermute | solution.py:21
  317.5 5.9 %collective-permute-start.30 = (bf16[4,128,128]{2,1,0:T(8,128)(2,1)S(1)}, bf16[4,128,128]{2,1,0:T(8,128)(2,1)S(1)}, u32[]{:S(2)}, u32[]{:S(2)}) collective-permute-start(bf16[4,128,128]{2,1,0:T(8,128)(2,1)S(1)} %pad_maximum_fusion), channel_id=1, source_target_pairs={{0,6},{2,4},{4,2},{6,0},{1,7},{3,5},{5,3},{7,1},{8,14},{10,12},{12... | collective-permute-start | bytes 393224 | tf_op jit(solution)/shard_map/ppermute | solution.py:23
  323.5 10.2 %collective-permute-start.31 = (bf16[16,128,128]{2,1,0:T(8,128)(2,1)S(1)}, bf16[16,128,128]{2,1,0:T(8,128)(2,1)S(1)}, u32[]{:S(2)}, u32[]{:S(2)}) collective-permute-start(bf16[16,128,128]{2,1,0:T(8,128)(2,1)S(1)} %get-tuple-element.15), channel_id=1, source_target_pairs={{0,1},{1,0},{2,3},{3,2},{4,5},{5,4},{6,7},{7,6},{8,9},{9,8},{10,11... | collective-permute-start | bytes 1572872 | tf_op jit(solution)/shard_map/ppermute | solution.py:21
  (14 other events, 532.8 us)

commit v2 on v1

v2 whole, which is shorter than its diff:
```python
import functools

import jax
import jax.numpy as jnp
from jax import lax
from jax.experimental import pallas as pl
from jax.experimental.pallas import tpu as pltpu
from jax.sharding import Mesh, PartitionSpec as P

SEQ_LEN = 128
LINE = 4

shift_scale = 0.1
tiny_value = 1e-06

f32 = jnp.float32
bf16 = jnp.bfloat16


def swap(value, axis):
    if isinstance(axis, str):
        return lax.ppermute(value, axis, [(0, 1), (1, 0)])
    count = 2 ** len(axis)
    return lax.ppermute(value, axis, [(i, count - 1 - i) for i in range(count)])


def settle(*values):
    return lax.optimization_barrier(values)


def dot_t(left, right):
    return lax.dot_general(left, right, (((1,), (1,)), ((), ())), preferred_element_type=f32)


class Columns:
    def __init__(self, array, slots):
        self.arrays, self.slots = (array,), slots

    def copies(self, refs, table, k, chunk):
        start = pl.multiple_of(table[self.slots[k]] * chunk, chunk)
        return [(None, refs[0].at[:, pl.ds(start, chunk)])]


class Quarters:
    def __init__(self, arrays, slots):
        self.arrays, self.slots = arrays, slots

    def copies(self, refs, table, k, chunk):
        start = pl.multiple_of(table[self.slots[k] + 1] * chunk, chunk)
        place = table[self.slots[k]]
        return [(place == n, ref.at[:, pl.ds(start, chunk)]) for n, ref in enumerate(refs)]


class Rows:
    def __init__(self, array, part):
        self.array, self.part = array, part


def start_one(choices, target, sem):
    for flag, ref in choices:
        copy = pltpu.make_async_copy(ref, target, sem)
        if flag is None:
            copy.start()
        else:
            pl.when(flag)(copy.start)
    return copy


def stage_kernel(plan, table, *refs):
    tiles, pieces, rows, chunk, has_total, tails = plan
    refs = list(refs)
    sources = [[refs.pop(0) for _ in tile.arrays] for tile in tiles]
    blocks = [[refs.pop(0) for _ in piece] for piece, _ in pieces]
    total_in = refs.pop(0) if has_total else None
    if tails:
        tail_refs = [[refs.pop(0) for _ in range(n)] for n in tails]
        proj_in = refs.pop(0)
    out, grads, weights, total, sems = [refs.pop(0) for _ in range(5)]
    if tails:
        tail_vmem, proj_vmem, tail_sems = refs
    units = weights.shape[1]
    inner = table[0] == 1

    waits = []
    if has_total:
        copy = pltpu.make_async_copy(total_in, total, sems.at[len(pieces), 0])
        copy.start()
        waits.append(copy)
    copies = []
    for k, block in enumerate(blocks):
        mine = []
        if pieces[k][1] is not None:
            block = [block[0].at[pl.ds(pieces[k][1] * units, units), :]]
        choices = [(None, block[0])]
        if len(block) > 1:
            choices = [(inner, block[0]), (jnp.logical_not(inner), block[1])]
        mine.append(start_one(choices, weights.at[k], sems.at[k, len(tiles)]))
        for t, tile in enumerate(tiles):
            mine.append(start_one(tile.copies(sources[t], table, k, chunk), grads.at[k, t], sems.at[k, t]))
        copies.append(mine)
    tail_copies = []
    if tails:
        copy = pltpu.make_async_copy(
            proj_in.at[:, pl.ds(pl.multiple_of(table[1], 128), units)], proj_vmem, tail_sems.at[len(tails), 0]
        )
        copy.start()
        tail_copies.append(copy)
        for t, pair in enumerate(tail_refs):
            for which in range(2):
                ref = pair[which] if len(pair) == 2 else pair[0].at[which]
                copy = pltpu.make_async_copy(ref, tail_vmem.at[t, which], tail_sems.at[t, which])
                copy.start()
                tail_copies.append(copy)
    for copy in waits:
        copy.wait()
    goal = out if not tails else total
    for k in range(len(pieces)):
        for copy in copies[k]:
            copy.wait()
        for t in range(len(tiles)):
            term = dot_t(grads[k, t], weights[k])
            where = pl.ds(t * rows, rows)
            if k > 0:
                goal[where, :] += term
            elif has_total:
                goal[where, :] = total[where, :] + term
            else:
                goal[where, :] = term
    if tails:
        for copy in tail_copies:
            copy.wait()
        for t in range(len(tiles)):
            where = pl.ds(t * rows, rows)
            wide = tail_vmem[t, 1].astype(f32)
            logistic = jax.nn.sigmoid(wide)
            scaled = total[where, :] * tail_vmem[t, 0].astype(f32) * logistic * (1.0 + wide * (1.0 - logistic))
            out[where, :] = dot_t(scaled.astype(bf16), proj_vmem[...])


def stage(table, tiles, pieces, rows, total=None, tails=None, proj=None):
    parts = [p.part if isinstance(p, Rows) else None for p in pieces]
    pieces = [p.array if isinstance(p, Rows) else p for p in pieces]
    pieces = [p if isinstance(p, tuple) else (p,) for p in pieces]
    units, chunk = pieces[0][0].shape
    units = units if parts[0] is None else units // 2
    operands = [v for tile in tiles for v in tile.arrays] + [v for p in pieces for v in p]
    width = units
    if total is not None:
        operands.append(total)
    scratch = [
        pltpu.VMEM((len(pieces), len(tiles), rows, chunk), bf16),
        pltpu.VMEM((len(pieces), units, chunk), bf16),
        pltpu.VMEM((len(tiles) * rows, units) if total is not None else (8, 128), f32),
        pltpu.SemaphoreType.DMA((len(pieces) + 1, len(tiles) + 1)),
    ]
    if tails is not None:
        tails = [tail if isinstance(tail, tuple) else (tail,) for tail in tails]
        operands += [v for tail in tails for v in tail] + [proj]
        width = proj.shape[0]
        scratch += [
            pltpu.VMEM((len(tiles), 2, rows, units), bf16),
            pltpu.VMEM((width, units), bf16),
            pltpu.SemaphoreType.DMA((len(tails) + 1, 2)),
        ]
    plan = (tiles, list(zip(pieces, parts)), rows, chunk, total is not None, [len(tail) for tail in tails] if tails else None)
    height = len(tiles) * rows
    return pl.pallas_call(
        functools.partial(stage_kernel, plan),
        out_shape=jax.ShapeDtypeStruct((height, width), f32),
        in_specs=[pl.BlockSpec(memory_space=pltpu.SMEM)] + [pl.BlockSpec(memory_space=pl.ANY)] * len(operands),
        out_specs=pl.BlockSpec(memory_space=pltpu.VMEM),
        scratch_shapes=scratch,
        compiler_params=pltpu.CompilerParams(vmem_limit_bytes=44 * 2**20),
        cost_estimate=pl.CostEstimate(
            flops=2 * height * units * chunk * len(pieces),
            bytes_accessed=4 * height * units,
            transcendentals=0,
        ),
    )(table, *operands)


def local(tokens, grad_out, gate_pre, up_value, down_weight, in_proj, out_proj, test_matrix):
    z, y, x, c = (lax.axis_index(a) for a in ("z", "y", "x", "c"))
    middle = lax.axis_size("m")
    rows, width = grad_out.shape
    pdim = in_proj.shape[0]
    chunk = down_weight.shape[1] * middle
    if middle > 1:
        down_weight = lax.all_gather(down_weight, "m", axis=1, tiled=True)
        grad_out = grad_out.reshape(rows, LINE, middle, 2, -1).swapaxes(2, 3).reshape(rows, -1)
    half = down_weight.shape[0] // 2
    moved = half * 5 // 14 // 128 * 128
    stay = half - moved
    inner = (z > 0) & (z < LINE - 1)
    PAIR = [(0, 1), (1, 0), (2, 3), (3, 2)]
    IN, OUT, ACROSS = [(0, 1), (3, 2)], [(1, 0), (2, 3)], [(1, 2), (2, 1)]

    def along(value, pairs):
        return lax.ppermute(value, "z", pairs)

    def cut(value, index, dim, kept):
        start = index * half + (moved if kept else 0)
        return lax.dynamic_slice_in_dim(value, start, stay if kept else moved, dim)

    def both_values(index, kept):
        return jnp.stack((cut(up_value, index, 1, kept), cut(gate_pre, index, 1, kept)))

    quarter = width // 4
    k_own = cut(down_weight, y, 0, True)
    k_near, k_mid = along(k_own, PAIR), along(k_own, ACROSS)
    kt_own = swap(cut(down_weight, 1 - y, 0, True), "y")
    o_own, ot_send = cut(down_weight, y, 0, False), cut(down_weight, 1 - y, 0, False)
    sent = lax.dynamic_slice_in_dim(grad_out, (x * 2 + c) * quarter, quarter, 1)
    values_o, values_os = both_values(y, False), both_values(1 - y, False)
    k_own, k_near, k_mid, kt_own, o_own, ot_send, sent, values_o, values_os = settle(
        k_own, k_near, k_mid, kt_own, o_own, ot_send, sent, values_o, values_os
    )

    kt_near, kt_mid = along(kt_own, PAIR), along(kt_own, ACROSS)
    sent_y = swap(sent, "y")
    values_k, values_ks = both_values(y, True), both_values(1 - y, True)
    kt_near, kt_mid, sent_y, values_k, values_ks, sent, k_mid, k_near, ot_send = settle(
        kt_near, kt_mid, sent_y, values_k, values_ks, sent, k_mid, k_near, ot_send
    )

    grads_e, k_second, k_far = along(sent, IN), along(k_mid, OUT), along(k_near, ACROSS)
    ot_own = swap(ot_send, "y")
    sent_yx = swap(sent_y, "x")
    act_part = dot_t(tokens, in_proj)
    values_ks0 = swap(values_ks[0], "y")
    grads_e, k_second, k_far, ot_own, sent_y, sent_yx, act_part, kt_mid, kt_near, o_own = settle(
        grads_e, k_second, k_far, ot_own, sent_y, sent_yx, act_part, kt_mid, kt_near, o_own
    )

    o_both = jnp.concatenate((o_own, ot_own), 0)
    o_end, kt_second, kt_far = along(o_both, IN), along(kt_mid, OUT), along(kt_near, ACROSS)
    grads_ey = swap(grads_e, "y")
    grads_ex = swap(grads_e, "x")
    grads_y = (sent_y, swap(sent_y, "c"), sent_yx, swap(sent_yx, "c"))
    (o_end, kt_second, kt_far, grads_e, grads_ex, grads_ey, o_both, k_far, values_o, values_os, values_ks0, values_ks) = settle(
        o_end, kt_second, kt_far, grads_e, grads_ex, grads_ey, o_both, k_far, values_o, values_os, values_ks0, values_ks
    )

    values_e, k_third, o_mid = along(values_o, IN), along(k_far, OUT), along(o_both, ACROSS)
    values_oy = swap(values_os, "y")
    grads_eyx = swap(grads_ey, "x")
    grads_far = [(grads_e, swap(grads_e, "c"), grads_ex, swap(grads_ex, "c"))]

    own = x * 2 + c
    near = jnp.where(z % 2 == 0, z + 1, z - 1)
    other = jnp.where(z < 2, 2, 1)
    far = jnp.where(z < 2, 3, 0)

    def table(start, *chunks):
        values = [inner.astype(jnp.int32), start]
        for at, side in chunks:
            at = at * 2 + side
            values += [at, (at // 2) ^ own, at % 2]
        return jnp.stack([jnp.asarray(v, jnp.int32) for v in values])

    def slots(count, skip):
        return [2 + 3 * k + skip for k in range(count)]

    yt = 1 - y
    first = ((z, y), (z, yt), (near, y), (near, yt), (other, y), (other, yt))
    last = ((far, y), (far, yt))
    table_first = table(0, *first)

    def near_tiles(n):
        return [Columns(grad_out, slots(n, 0)), Quarters(grads_y, slots(n, 1))]

    def far_tiles(n):
        return [Quarters(arrays, slots(n, 1)) for arrays in grads_far]

    k_pieces = [k_own, kt_own, k_near, kt_near, (k_mid, k_second), (kt_mid, kt_second)]
    k_total = stage(table_first, near_tiles(6), k_pieces, rows)
    (values_e, k_third, o_mid, values_oy, grads_ey, grads_eyx, k_total, o_end, kt_far, values_ks) = settle(
        values_e, k_third, o_mid, values_oy, grads_ey, grads_eyx, k_total, o_end, kt_far, values_ks
    )

    values_ey, kt_third, o_far = along(values_oy, IN), along(kt_far, OUT), along(o_end, ACROSS)
    values_ks1 = swap(values_ks[1], "y")
    values_ky = (values_ks0, values_ks1)
    grads_far.append((grads_ey, swap(grads_ey, "c"), grads_eyx, swap(grads_eyx, "c")))
    o_total = stage(table_first, near_tiles(6) + far_tiles(6), [o_own, ot_own, Rows(o_end, 0), Rows(o_end, 1), Rows(o_mid, 0), Rows(o_mid, 1)], rows)
    o_total, values_ey, kt_third, o_far = settle(o_total, values_ey, kt_third, o_far)
    out_k = stage(
        table(y * half + moved, *last), near_tiles(2), [(k_far, k_third), (kt_far, kt_third)], rows, k_total,
        [values_k, values_ky], out_proj,
    )
    out_o = stage(
        table(y * half, *last), near_tiles(2) + far_tiles(2), [Rows(o_far, 0), Rows(o_far, 1)], rows, o_total,
        [values_o, values_oy, values_e, values_ey], out_proj,
    )

    act_blocks = act_part.reshape(2, 2, SEQ_LEN, pdim)
    act_kept = lax.dynamic_index_in_dim(act_blocks, c, 1, False) + swap(
        lax.dynamic_index_in_dim(act_blocks, 1 - c, 1, False), "c"
    )
    act_seq = (
        lax.dynamic_index_in_dim(act_kept, x, 0, False)
        + swap(lax.dynamic_index_in_dim(act_kept, 1 - x, 0, False), "x")
    ).astype(bf16)

    out_o = out_o.reshape(2, 2 * rows, pdim)
    blocks = jnp.stack((out_k + jnp.where(inner, out_o[0], 0.0), out_o[1])).reshape(2, 2, 2, 2, SEQ_LEN, pdim)
    kept = lax.dynamic_index_in_dim(blocks, c, 3, False) + swap(
        lax.dynamic_index_in_dim(blocks, 1 - c, 3, False), "c"
    )
    own_x = lax.dynamic_index_in_dim(kept, x, 2, False)
    other_x = lax.dynamic_index_in_dim(kept, 1 - x, 2, False)
    out_sum = own_x[:, 0] + swap(other_x[:, 0], "x") + swap(own_x[:, 1], "y") + swap(other_x[:, 1], ("y", "x"))
    out_seq = (out_sum[0] + lax.ppermute(out_sum[1], "z", [(1, 0), (2, 3)])).astype(bf16)

    proj_own = lax.dot_general(
        act_seq, out_seq, (((0,), (0,)), ((), ())), preferred_element_type=f32
    ).astype(bf16)
    gathered = [proj_own] + [
        lax.ppermute(proj_own, "z", [(i, (i + d) % LINE) for i in range(LINE)]) for d in range(1, LINE)
    ]
    gathered = jnp.stack(gathered)
    if middle > 1:
        gathered = lax.all_gather(gathered, "m", axis=0, tiled=True)
    gathered = jnp.concatenate((gathered, swap(gathered, "x"), swap(gathered, "y"), swap(gathered, ("y", "x"))), 0)
    gathered = jnp.concatenate((gathered, swap(gathered, "c")), 0)
    seqs = gathered.shape[0]
    proj_grad = gathered.reshape(seqs, pdim * pdim)

    own_index = lax.axis_index(("z", "m", "y", "x", "c"))
    own_width = pdim * pdim // (LINE * middle * 8)
    gram = lax.dot_general(
        test_matrix, test_matrix, (((0,), (0,)), ((), ())), preferred_element_type=f32
    )
    omega_sq = jnp.trace(gram)
    coeff_wide = jnp.dot(proj_grad, test_matrix, preferred_element_type=f32)
    coeff = coeff_wide.astype(bf16)
    overlap = dot_t(proj_grad, proj_grad)
    coeff_up = coeff.astype(f32)
    pairs = lax.dot_general(coeff_up, coeff_up, (((1,), (1,)), ((), ())), precision=lax.Precision.HIGHEST)
    square_sum = jnp.sum(overlap * pairs)
    core_sketch = lax.dot_general(
        coeff_wide, coeff_up, (((0,), (0,)), ((), ())), precision=lax.Precision.HIGHEST
    )
    own_rows = lax.dot_general(
        lax.dynamic_slice_in_dim(proj_grad, own_index * own_width, own_width, 1), coeff,
        (((0,), (0,)), ((), ())), preferred_element_type=f32,
    )
    shift = shift_scale * jnp.sqrt(square_sum / (omega_sq + tiny_value))
    core = core_sketch + shift * gram
    core = 0.5 * (core + core.T)
    lower = jnp.linalg.cholesky(core)
    omega_own = lax.dynamic_slice_in_dim(test_matrix, own_index * own_width, own_width, 0).astype(f32)
    shifted = own_rows + shift * omega_own
    return jax.scipy.linalg.solve_triangular(lower, shifted.T, lower=True).T


def solution(mesh):
    dp, tensor = mesh.shape["dp"], mesh.shape["tensor"]
    grid = Mesh(
        mesh.devices.reshape(LINE, dp // (2 * LINE), 2, tensor // 2, 2), ("z", "m", "y", "x", "c")
    )
    dps, tensors = ("z", "m", "y"), ("x", "c")
    in_specs = (
        P(dps, tensors),
        P(dps, None),
        P(dps, tensors),
        P(dps, tensors),
        P(tensors, dps),
        P(None, tensors),
        P(None, tensors),
        P(),
    )
    out_specs = P(dps + tensors, None)
    return jax.shard_map(local, mesh=grid, in_specs=in_specs, out_specs=out_specs, check_vma=False)
```

time: 367 us -> 306 us (0.83); the launches traced: 367 us -> 300 us
  matrix products: 91.4 us -> 9.46 us
  waiting for transfers between devices: 170 us -> 113 us
  Pallas kernels: 0 us -> 46.9 us
  starting transfers between devices: 57.7 us -> 72.2 us
  local copies, waits for them, and re-layouts: 22.3 us -> 28.4 us
  other arithmetic: 22.9 us -> 27.6 us
    ppermute x15 -> x20, waiting for transfers between devices: 133 us -> 38.9 us  [the longest x16 31.6 us: along(): return lax.ppermute(value, 'z', pairs)]
    dot_general x12 -> x2, matrix products: 80 us -> 1.8 us  [dot_t(): lax.dot_general(left, right, (((1,), (1,)), ((), ())), preferred_element_...]
    pallas_call x0 -> x4, Pallas kernels: none -> 46.9 us  [stage(): pl.pallas_call(functools.partial(stage_kernel, plan), out_shape=jax.Shape...]
    ppermute x15 -> x24, waiting for transfers between devices: 34.1 us -> 69.4 us  [swap(): return lax.ppermute(value, axis, [(0, 1), (1, 0)])]
    unnamed x42 -> x85, local copies, waits for them, and re-layouts: 4.89 us -> 16.8 us
    ppermute x15 -> x20, starting transfers between devices: 41.2 us -> 49.4 us  [the longest x16 44.1 us: along(): return lax.ppermute(value, 'z', pairs)]
    ppermute x15 -> x24, starting transfers between devices: 12.8 us -> 19.8 us  [swap(): return lax.ppermute(value, axis, [(0, 1), (1, 0)])]
    another operation x0 -> x5, other arithmetic: none -> 4.49 us  [the longest x4 4.39 us: both_values(): jnp.stack((cut(up_value, index, 1, kept), cut(gate_pre, index, 1, kept)))]
  transfers between devices with their start and end apart: 32 -> 46, of which waited for: 18 -> 24; matrix products, arithmetic and copies ran while one was open for 27% -> 5% of each run, Pallas kernels for 0% -> 13%
where the time goes in v2:
time: 306 us; the launch traced here: 300 us
  waiting for transfers between devices  113 us (37%)
  starting transfers between devices  72.2 us (24%)
  Pallas kernels  46.9 us (15%)
  local copies, waits for them, and re-layouts  28.4 us (9%)
  other arithmetic  27.6 us (9%)
  matrix products  9.46 us (3%)
    ppermute x24, waiting for transfers between devices, swap(): return lax.ppermute(value, axis, [(0, 1), (1, 0)])  69.4 us
    pallas_call x4, Pallas kernels, stage(): pl.pallas_call(functools.partial(stage_kernel, plan), out_shape=jax.Shape...  46.9 us
    ppermute x16, starting transfers between devices, along(): return lax.ppermute(value, 'z', pairs)  44.1 us
    ppermute x16, waiting for transfers between devices, along(): return lax.ppermute(value, 'z', pairs)  31.6 us
    ppermute x24, starting transfers between devices, swap(): return lax.ppermute(value, axis, [(0, 1), (1, 0)])  19.8 us
    unnamed x85, local copies, waits for them, and re-layouts  16.8 us
    another operation x3, other arithmetic, local(): lower = jnp.linalg.cholesky(core)  12.4 us
    another operation x2, other arithmetic, local(): return jax.scipy.linalg.solve_triangular(lower, shifted.T, lower=True).T  10.5 us
  transfers between devices with their start and end apart: 46, of which 24 were waited for; matrix products, arithmetic and copies ran while one was open for 5% of the time, Pallas kernels for 13%

profile of v2, /device:TPU:0, one launch (start us, length us, event | category | flops | bytes accessed | tf_op | source)
XLA Modules:
  0.0 300.1 jit_solution(7808268933862306952)
XLA Ops:
  0.0 2.9 constant_dynamic-slice_fusion.3
  2.9 3.0 %collective-permute-start = (bf16[1152,512]{1,0:T(8,128)(2,1)S(1)}, bf16[1152,512]{1,0:T(8,128)(2,1)}, u32[]{:S(2)}, u32[]{:S(2)}) collective-permute-start(bf16[1152,512]{1,0:T(8,128)(2,1)S(1)} %get-tuple-element.89.refs_5_), channel_id=1, source_target_pairs={{0,8},{8,0},{16,24},{24,16},{1,9},{9,1},{17,25},{25,17},{2,10},{10... | collective-permute-start | bytes 3538952 | tf_op jit(solution)/shard_map/ppermute | solution.py:199
  12.0 1.8 dynamic-slice_bitcast_fusion.4
  16.2 15.8 %collective-permute-done.refs_7_ = bf16[1152,512]{1,0:T(8,128)(2,1)} collective-permute-done((bf16[1152,512]{1,0:T(8,128)(2,1)S(1)}, bf16[1152,512]{1,0:T(8,128)(2,1)}, u32[]{:S(2)}, u32[]{:S(2)}) %collective-permute-start) | collective-permute-done | bytes 1179680 | tf_op jit(solution)/shard_map/ppermute | solution.py:199
  32.0 3.3 %collective-permute-done.2.refs_6_ = bf16[1152,512]{1,0:T(8,128)(2,1)} collective-permute-done((bf16[1152,512]{1,0:T(8,128)(2,1)}, bf16[1152,512]{1,0:T(8,128)(2,1)}, u32[]{:S(2)}, u32[]{:S(2)}) %collective-permute-start.2) | collective-permute-done | bytes 1179680 | tf_op jit(solution)/shard_map/ppermute | solution.py:22
  35.4 3.2 %collective-permute-start.3 = (bf16[1152,512]{1,0:T(8,128)(2,1)}, bf16[1152,512]{1,0:T(8,128)(2,1)S(1)}, u32[]{:S(2)}, u32[]{:S(2)}) collective-permute-start(bf16[1152,512]{1,0:T(8,128)(2,1)} %collective-permute-done.2.refs_6_), channel_id=1, source_target_pairs={{0,8},{8,0},{16,24},{24,16},{1,9},{9,1},{17,25},{25,17},{2,10},{10... | collective-permute-start | bytes 3538952 | tf_op jit(solution)/shard_map/ppermute | solution.py:199
  43.2 19.2 %collective-permute-done.5.refs_1_ = bf16[512,1024]{1,0:T(8,128)(2,1)S(1)} collective-permute-done((bf16[512,1024]{1,0:T(8,128)(2,1)S(1)}, bf16[512,1024]{1,0:T(8,128)(2,1)S(1)}, u32[]{:S(2)}, u32[]{:S(2)}) %collective-permute-start.5) | collective-permute-done | bytes 1048608 | tf_op jit(solution)/shard_map/ppermute | solution.py:22
  69.3 6.4 %collective-permute-start.6 = (bf16[512,1024]{1,0:T(8,128)(2,1)S(1)}, bf16[512,1024]{1,0:T(8,128)(2,1)S(1)}, u32[]{:S(2)}, u32[]{:S(2)}) collective-permute-start(bf16[512,1024]{1,0:T(8,128)(2,1)S(1)} %constant_dynamic-slice_fusion), channel_id=1, source_target_pairs={{0,8},{24,16},{1,9},{25,17},{2,10},{26,18},{3,11},{27,19},{4,12},{... | collective-permute-start | bytes 3145736 | tf_op jit(solution)/shard_map/ppermute | solution.py:199
  75.9 2.3 collective-permute-done.9.refs_14_
  80.2 10.2 %collective-permute-done.10.refs_3_ = bf16[512,1024]{1,0:T(8,128)(2,1)S(1)} collective-permute-done((bf16[512,1024]{1,0:T(8,128)(2,1)S(1)}, bf16[512,1024]{1,0:T(8,128)(2,1)S(1)}, u32[]{:S(2)}, u32[]{:S(2)}) %collective-permute-start.10) | collective-permute-done | bytes 1048608 | tf_op jit(solution)/shard_map/ppermute | solution.py:22
  90.3 4.7 %collective-permute-done.6.refs_5_ = bf16[512,1024]{1,0:T(8,128)(2,1)S(1)} collective-permute-done((bf16[512,1024]{1,0:T(8,128)(2,1)S(1)}, bf16[512,1024]{1,0:T(8,128)(2,1)S(1)}, u32[]{:S(2)}, u32[]{:S(2)}) %collective-permute-start.6) | collective-permute-done | bytes 1048608 | tf_op jit(solution)/shard_map/ppermute | solution.py:199
  97.9 5.8 %collective-permute-start.15 = (bf16[1280,512]{1,0:T(8,128)(2,1)}, bf16[1280,512]{1,0:T(8,128)(2,1)}, u32[]{:S(2)}, u32[]{:S(2)}) collective-permute-start(bf16[1280,512]{1,0:T(8,128)(2,1)} %constant_dynamic-update-slice_fusion), channel_id=1, source_target_pairs={{0,8},{24,16},{1,9},{25,17},{2,10},{26,18},{3,11},{27,19},{4,12},{... | collective-permute-start | bytes 3932168 | tf_op jit(solution)/shard_map/ppermute | solution.py:199
  105.0 2.1 collective-permute-done.20.refs_11_
  108.8 7.3 %collective-permute-done.18.refs_7_ = bf16[512,1024]{1,0:T(8,128)(2,1)} collective-permute-done((bf16[512,1024]{1,0:T(8,128)(2,1)S(1)}, bf16[512,1024]{1,0:T(8,128)(2,1)}, u32[]{:S(2)}, u32[]{:S(2)}) %collective-permute-start.18) | collective-permute-done | bytes 1048608 | tf_op jit(solution)/shard_map/ppermute | solution.py:22
  116.1 9.4 %collective-permute-done.19.refs_9_ = bf16[512,1024]{1,0:T(8,128)(2,1)} collective-permute-done((bf16[512,1024]{1,0:T(8,128)(2,1)S(1)}, bf16[512,1024]{1,0:T(8,128)(2,1)}, u32[]{:S(2)}, u32[]{:S(2)}) %collective-permute-start.19) | collective-permute-done | bytes 1048608 | tf_op jit(solution)/shard_map/ppermute | solution.py:22
  125.5 3.4 %collective-permute-done.16.refs_12_ = bf16[1152,512]{1,0:T(8,128)(2,1)S(1)} collective-permute-done((bf16[1152,512]{1,0:T(8,128)(2,1)S(1)}, bf16[1152,512]{1,0:T(8,128)(2,1)S(1)}, u32[]{:S(2)}, u32[]{:S(2)}) %collective-permute-start.16) | collective-permute-done | bytes 1179680 | tf_op jit(solution)/shard_map/ppermute | solution.py:199
  131.1 7.8 %collective-permute-start.21 = (bf16[2,512,640]{2,1,0:T(8,128)(2,1)}, bf16[2,512,640]{2,1,0:T(8,128)(2,1)}, u32[]{:S(2)}, u32[]{:S(2)}) collective-permute-start(bf16[2,512,640]{2,1,0:T(8,128)(2,1)} %pad_maximum_fusion.2.refs_16_), channel_id=1, source_target_pairs={{0,8},{24,16},{1,9},{25,17},{2,10},{26,18},{3,11},{27,19},{4,12},{... | collective-permute-start | bytes 3932168 | tf_op jit(solution)/shard_map/ppermute | solution.py:199
  143.2 9.6 %collective-permute-done.25.refs_11_ = bf16[512,1024]{1,0:T(8,128)(2,1)} collective-permute-done((bf16[512,1024]{1,0:T(8,128)(2,1)}, bf16[512,1024]{1,0:T(8,128)(2,1)}, u32[]{:S(2)}, u32[]{:S(2)}) %collective-permute-start.25) | collective-permute-done | bytes 1048608 | tf_op jit(solution)/shard_map/ppermute | solution.py:22
  152.8 4.3 %collective-permute-done.22.refs_6_ = bf16[1152,512]{1,0:T(8,128)(2,1)} collective-permute-done((bf16[1152,512]{1,0:T(8,128)(2,1)}, bf16[1152,512]{1,0:T(8,128)(2,1)}, u32[]{:S(2)}, u32[]{:S(2)}) %collective-permute-start.22) | collective-permute-done | bytes 1179680 | tf_op jit(solution)/shard_map/ppermute | solution.py:199
  160.8 13.4 %shard_map.82.refs_9_ = f32[1024,1152]{1,0:T(8,128)} custom-call(s32[20]{0:T(128)S(1)} %stack.200.table, bf16[512,4096]{1,0:T(8,128)(2,1)} %refs_0_.7, bf16[512,1024]{1,0:T(8,128)(2,1)S(1)} %collective-permute-done.5.refs_1_, bf16[512,1024]{1,0:T(8,128)(2,1)S(1)} %collective-permute-done.13.refs_2_, bf16[512,1024]{1,0:T(8,128)(2,1)S(1)} %collective-permute-done.10.refs_3_, ...), custom_call_target="tpu_custom_call" | custom-call | flops 7247757312 | bytes 4718592 | tf_op jit(solution)/shard_map/pallas_call | solution.py:167
  174.9 3.4 %collective-permute-start.30 = (bf16[2,512,640]{2,1,0:T(8,128)(2,1)}, bf16[2,512,640]{2,1,0:T(8,128)(2,1)}, u32[]{:S(2)}, u32[]{:S(2)}) collective-permute-start(bf16[2,512,640]{2,1,0:T(8,128)(2,1)} %collective-permute-done.24.refs_17_), channel_id=1, source_target_pairs={{0,8},{24,16},{1,9},{25,17},{2,10},{26,18},{3,11},{27,19},{4,12},{... | collective-permute-start | bytes 3932168 | tf_op jit(solution)/shard_map/ppermute | solution.py:199
  193.2 16.0 %shard_map.83.refs_15_ = f32[2048,640]{1,0:T(8,128)} custom-call(s32[20]{0:T(128)S(1)} %stack.200.table, bf16[512,4096]{1,0:T(8,128)(2,1)} %refs_0_.7, bf16[512,1024]{1,0:T(8,128)(2,1)S(1)} %collective-permute-done.5.refs_1_, bf16[512,1024]{1,0:T(8,128)(2,1)S(1)} %collective-permute-done.13.refs_2_, bf16[512,1024]{1,0:T(8,128)(2,1)S(1)} %collective-permute-done.10.refs_3_, ...), custom_call_target="tpu_custom_call" | custom-call | flops 8053063680 | bytes 5242880 | tf_op jit(solution)/shard_map/pallas_call | solution.py:167
  209.2 2.7 collective-permute-done.31.refs_8_
  211.9 9.3 %shard_map.85 = f32[2048,128]{1,0:T(8,128)S(1)} custom-call(s32[8]{0:T(128)S(1)} %stack.202.table, bf16[512,4096]{1,0:T(8,128)(2,1)} %refs_0_.7, bf16[512,1024]{1,0:T(8,128)(2,1)S(1)} %collective-permute-done.5.refs_1_, bf16[512,1024]{1,0:T(8,128)(2,1)S(1)} %collective-permute-done.13.refs_2_, bf16[512,1024]{1,0:T(8,128)(2,1)S(1)} %collective-permute-done.10.refs_3_, ...), custom_call_target="tpu_custom_call" | custom-call | flops 2684354560 | bytes 5242880 | tf_op jit(solution)/shard_map/pallas_call | solution.py:167
  221.3 8.2 %shard_map.84 = f32[1024,128]{1,0:T(8,128)S(1)} custom-call(s32[8]{0:T(128)S(1)} %stack.181.table, bf16[512,4096]{1,0:T(8,128)(2,1)} %refs_0_.7, bf16[512,1024]{1,0:T(8,128)(2,1)S(1)} %collective-permute-done.5.refs_1_, bf16[512,1024]{1,0:T(8,128)(2,1)S(1)} %collective-permute-done.13.refs_2_, bf16[512,1024]{1,0:T(8,128)(2,1)S(1)} %collective-permute-done.10.refs_3_, ...), custom_call_target="tpu_custom_call" | custom-call | flops 2415919104 | bytes 4718592 | tf_op jit(solution)/shard_map/pallas_call | solution.py:167
  238.1 3.9 %collective-permute-done.37 = f32[2,128,128]{2,1,0:T(8,128)S(1)} collective-permute-done((f32[2,128,128]{2,1,0:T(8,128)S(1)}, f32[2,128,128]{2,1,0:T(8,128)S(1)}, u32[]{:S(2)}, u32[]{:S(2)}) %collective-permute-start.37) | collective-permute-done | bytes 131104 | tf_op jit(solution)/shard_map/ppermute | solution.py:24
  244.1 4.8 %collective-permute-done.38 = f32[128,128]{1,0:T(8,128)S(1)} collective-permute-done((f32[128,128]{1,0:T(8,128)S(1)}, f32[128,128]{1,0:T(8,128)S(1)}, u32[]{:S(2)}, u32[]{:S(2)}) %collective-permute-start.38) | collective-permute-done | bytes 65568 | tf_op jit(solution)/shard_map/ppermute | solution.py:313
  249.3 2.2 collective-permute-start.40
  264.7 1.9 select_reduce_fusion.1
  269.2 3.0 %fusion.30 = f32[32,128]{1,0:T(8,128)S(1)} fusion(bf16[32,16384]{1,0:T(8,128)(2,1)S(1)} %concatenate.41, bf16[16384,128]{1,0:T(8,128)(2,1)} %param.15), kind=kOutput, calls=%fused_computation.101 | convolution fusion | flops 134217728 | bytes 5259264 | tf_op jit(solution)/shard_map/dot_general | solution.py:335
  274.8 11.7 %cholesky.13 = f32[128,128]{1,0:T(8,128)S(1)} custom-call(f32[128,128]{1,0:T(8,128)S(1)} %fusion.17), custom_call_target="Cholesky" | custom-call | tf_op jit(solution)/shard_map/jit(cholesky)/cholesky | solution.py:351
  287.9 9.8 %custom-call.7 = f32[1,128,128]{1,2,0:T(8,128)S(1)} custom-call(f32[1,128,128]{2,1,0:T(8,128)S(1)} %fusion.11), custom_call_target="InvertDiagBlocksLowerTriangular" | custom-call | tf_op jit(solution)/shard_map/jit(_solve_triangular)/triangular_solve | solution.py:354
  (196 shorter events, 85.1 us)
Async XLA Ops:
  2.9 29.1 %collective-permute-start = (bf16[1152,512]{1,0:T(8,128)(2,1)S(1)}, bf16[1152,512]{1,0:T(8,128)(2,1)}, u32[]{:S(2)}, u32[]{:S(2)}) collective-permute-start(bf16[1152,512]{1,0:T(8,128)(2,1)S(1)} %get-tuple-element.89.refs_5_), channel_id=1, source_target_pairs={{0,8},{8,0},{16,24},{24,16},{1,9},{9,1},{17,25},{25,17},{2,10},{10... | collective-permute-start | bytes 3538952 | tf_op jit(solution)/shard_map/ppermute | solution.py:199
  5.9 26.1 %collective-permute-start.1 = (bf16[1152,512]{1,0:T(8,128)(2,1)S(1)}, bf16[1152,512]{1,0:T(8,128)(2,1)}, u32[]{:S(2)}, u32[]{:S(2)}) collective-permute-start(bf16[1152,512]{1,0:T(8,128)(2,1)S(1)} %get-tuple-element.89.refs_5_), channel_id=1, source_target_pairs={{8,16},{16,8},{9,17},{17,9},{10,18},{18,10},{11,19},{19,11},{12,20... | collective-permute-start | bytes 3538952 | tf_op jit(solution)/shard_map/ppermute | solution.py:199
  7.6 27.7 %collective-permute-start.2 = (bf16[1152,512]{1,0:T(8,128)(2,1)}, bf16[1152,512]{1,0:T(8,128)(2,1)}, u32[]{:S(2)}, u32[]{:S(2)}) collective-permute-start(bf16[1152,512]{1,0:T(8,128)(2,1)} %get-tuple-element.123), channel_id=1, source_target_pairs={{0,4},{4,0},{1,5},{5,1},{2,6},{6,2},{3,7},{7,3},{8,12},{12,8},{9,1... | collective-permute-start | bytes 3538952 | tf_op jit(solution)/shard_map/ppermute | solution.py:22
  35.4 27.9 %collective-permute-start.3 = (bf16[1152,512]{1,0:T(8,128)(2,1)}, bf16[1152,512]{1,0:T(8,128)(2,1)S(1)}, u32[]{:S(2)}, u32[]{:S(2)}) collective-permute-start(bf16[1152,512]{1,0:T(8,128)(2,1)} %collective-permute-done.2.refs_6_), channel_id=1, source_target_pairs={{0,8},{8,0},{16,24},{24,16},{1,9},{9,1},{17,25},{25,17},{2,10},{10... | collective-permute-start | bytes 3538952 | tf_op jit(solution)/shard_map/ppermute | solution.py:199
  38.5 24.7 %collective-permute-start.4 = (bf16[1152,512]{1,0:T(8,128)(2,1)}, bf16[1152,512]{1,0:T(8,128)(2,1)S(1)}, u32[]{:S(2)}, u32[]{:S(2)}) collective-permute-start(bf16[1152,512]{1,0:T(8,128)(2,1)} %collective-permute-done.2.refs_6_), channel_id=1, source_target_pairs={{8,16},{16,8},{9,17},{17,9},{10,18},{18,10},{11,19},{19,11},{12,20... | collective-permute-start | bytes 3538952 | tf_op jit(solution)/shard_map/ppermute | solution.py:199
  39.3 23.2 %collective-permute-start.5 = (bf16[512,1024]{1,0:T(8,128)(2,1)S(1)}, bf16[512,1024]{1,0:T(8,128)(2,1)S(1)}, u32[]{:S(2)}, u32[]{:S(2)}) collective-permute-start(bf16[512,1024]{1,0:T(8,128)(2,1)S(1)} %constant_dynamic-slice_fusion), channel_id=1, source_target_pairs={{0,4},{4,0},{1,5},{5,1},{2,6},{6,2},{3,7},{7,3},{8,12},{12,8},{9,1... | collective-permute-start | bytes 3145736 | tf_op jit(solution)/shard_map/ppermute | solution.py:22
  63.2 15.0 %collective-permute-start.9 = (bf16[640,512]{1,0:T(8,128)(2,1)S(1)}, bf16[640,512]{1,0:T(8,128)(2,1)S(1)}, u32[]{:S(2)}, u32[]{:S(2)}) collective-permute-start(bf16[640,512]{1,0:T(8,128)(2,1)S(1)} %get-tuple-element.67), channel_id=1, source_target_pairs={{0,4},{4,0},{1,5},{5,1},{2,6},{6,2},{3,7},{7,3},{8,12},{12,8},{9,1... | collective-permute-start | bytes 1966088 | tf_op jit(solution)/shard_map/ppermute | solution.py:22
  64.8 30.2 %collective-permute-start.7 = (bf16[1152,512]{1,0:T(8,128)(2,1)}, bf16[1152,512]{1,0:T(8,128)(2,1)S(1)}, u32[]{:S(2)}, u32[]{:S(2)}) collective-permute-start(bf16[1152,512]{1,0:T(8,128)(2,1)} %collective-permute-done.1.refs_9_), channel_id=1, source_target_pairs={{8,0},{16,24},{9,1},{17,25},{10,2},{18,26},{11,3},{19,27},{12,4},{... | collective-permute-start | bytes 3538952 | tf_op jit(solution)/shard_map/ppermute | solution.py:199
  66.1 28.9 %collective-permute-start.8 = (bf16[1152,512]{1,0:T(8,128)(2,1)}, bf16[1152,512]{1,0:T(8,128)(2,1)}, u32[]{:S(2)}, u32[]{:S(2)}) collective-permute-start(bf16[1152,512]{1,0:T(8,128)(2,1)} %collective-permute-done.refs_7_), channel_id=1, source_target_pairs={{8,16},{16,8},{9,17},{17,9},{10,18},{18,10},{11,19},{19,11},{12,20... | collective-permute-start | bytes 3538952 | tf_op jit(solution)/shard_map/ppermute | solution.py:199
  67.8 22.5 %collective-permute-start.10 = (bf16[512,1024]{1,0:T(8,128)(2,1)S(1)}, bf16[512,1024]{1,0:T(8,128)(2,1)S(1)}, u32[]{:S(2)}, u32[]{:S(2)}) collective-permute-start(bf16[512,1024]{1,0:T(8,128)(2,1)S(1)} %collective-permute-done.5.refs_1_), channel_id=1, source_target_pairs={{0,2},{2,0},{1,3},{3,1},{4,6},{6,4},{5,7},{7,5},{8,10},{10,8},{9,1... | collective-permute-start | bytes 3145736 | tf_op jit(solution)/shard_map/ppermute | solution.py:22
  69.3 25.7 %collective-permute-start.6 = (bf16[512,1024]{1,0:T(8,128)(2,1)S(1)}, bf16[512,1024]{1,0:T(8,128)(2,1)S(1)}, u32[]{:S(2)}, u32[]{:S(2)}) collective-permute-start(bf16[512,1024]{1,0:T(8,128)(2,1)S(1)} %constant_dynamic-slice_fusion), channel_id=1, source_target_pairs={{0,8},{24,16},{1,9},{25,17},{2,10},{26,18},{3,11},{27,19},{4,12},{... | collective-permute-start | bytes 3145736 | tf_op jit(solution)/shard_map/ppermute | solution.py:199
  78.2 28.9 %collective-permute-start.20 = (bf16[512,1152]{1,0:T(8,128)(2,1)S(1)}, bf16[512,1152]{1,0:T(8,128)(2,1)S(1)}, u32[]{:S(2)}, u32[]{:S(2)}) collective-permute-start(bf16[512,1152]{1,0:T(8,128)(2,1)S(1)} %slice_bitcast_fusion.1), channel_id=1, source_target_pairs={{0,4},{4,0},{1,5},{5,1},{2,6},{6,2},{3,7},{7,3},{8,12},{12,8},{9,1... | collective-permute-start | bytes 3538952 | tf_op jit(solution)/shard_map/ppermute | solution.py:22
  95.0 21.1 %collective-permute-start.18 = (bf16[512,1024]{1,0:T(8,128)(2,1)S(1)}, bf16[512,1024]{1,0:T(8,128)(2,1)}, u32[]{:S(2)}, u32[]{:S(2)}) collective-permute-start(bf16[512,1024]{1,0:T(8,128)(2,1)S(1)} %collective-permute-done.6.refs_5_), channel_id=1, source_target_pairs={{0,2},{2,0},{1,3},{3,1},{4,6},{6,4},{5,7},{7,5},{8,10},{10,8},{9,1... | collective-permute-start | bytes 3145736 | tf_op jit(solution)/shard_map/ppermute | solution.py:22
  95.6 29.9 %collective-permute-start.19 = (bf16[512,1024]{1,0:T(8,128)(2,1)S(1)}, bf16[512,1024]{1,0:T(8,128)(2,1)}, u32[]{:S(2)}, u32[]{:S(2)}) collective-permute-start(bf16[512,1024]{1,0:T(8,128)(2,1)S(1)} %collective-permute-done.6.refs_5_), channel_id=1, source_target_pairs={{0,4},{4,0},{1,5},{5,1},{2,6},{6,2},{3,7},{7,3},{8,12},{12,8},{9,1... | collective-permute-start | bytes 3145736 | tf_op jit(solution)/shard_map/ppermute | solution.py:22
  97.9 31.0 %collective-permute-start.15 = (bf16[1280,512]{1,0:T(8,128)(2,1)}, bf16[1280,512]{1,0:T(8,128)(2,1)}, u32[]{:S(2)}, u32[]{:S(2)}) collective-permute-start(bf16[1280,512]{1,0:T(8,128)(2,1)} %constant_dynamic-update-slice_fusion), channel_id=1, source_target_pairs={{0,8},{24,16},{1,9},{25,17},{2,10},{26,18},{3,11},{27,19},{4,12},{... | collective-permute-start | bytes 3932168 | tf_op jit(solution)/shard_map/ppermute | solution.py:199
  103.7 25.1 %collective-permute-start.16 = (bf16[1152,512]{1,0:T(8,128)(2,1)S(1)}, bf16[1152,512]{1,0:T(8,128)(2,1)S(1)}, u32[]{:S(2)}, u32[]{:S(2)}) collective-permute-start(bf16[1152,512]{1,0:T(8,128)(2,1)S(1)} %collective-permute-done.4.refs_11_), channel_id=1, source_target_pairs={{8,0},{16,24},{9,1},{17,25},{10,2},{18,26},{11,3},{19,27},{12,4},{... | collective-permute-start | bytes 3538952 | tf_op jit(solution)/shard_map/ppermute | solution.py:199
  107.1 21.8 %collective-permute-start.17 = (bf16[1152,512]{1,0:T(8,128)(2,1)S(1)}, bf16[1152,512]{1,0:T(8,128)(2,1)}, u32[]{:S(2)}, u32[]{:S(2)}) collective-permute-start(bf16[1152,512]{1,0:T(8,128)(2,1)S(1)} %collective-permute-done.3.refs_8_), channel_id=1, source_target_pairs={{8,16},{16,8},{9,17},{17,9},{10,18},{18,10},{11,19},{19,11},{12,20... | collective-permute-start | bytes 3538952 | tf_op jit(solution)/shard_map/ppermute | solution.py:199
  116.1 22.8 %collective-permute-start.13 = (bf16[512,1024]{1,0:T(8,128)(2,1)S(1)}, bf16[512,1024]{1,0:T(8,128)(2,1)S(1)}, u32[]{:S(2)}, u32[]{:S(2)}) collective-permute-start(bf16[512,1024]{1,0:T(8,128)(2,1)S(1)} %collective-permute-done.5.refs_1_), channel_id=1, source_target_pairs={{0,1},{1,0},{2,3},{3,2},{4,5},{5,4},{6,7},{7,6},{8,9},{9,8},{10,11... | collective-permute-start | bytes 3145736 | tf_op jit(solution)/shard_map/ppermute | solution.py:22
  125.5 15.1 %collective-permute-start.14 = (bf16[512,1024]{1,0:T(8,128)(2,1)S(1)}, bf16[512,1024]{1,0:T(8,128)(2,1)S(1)}, u32[]{:S(2)}, u32[]{:S(2)}) collective-permute-start(bf16[512,1024]{1,0:T(8,128)(2,1)S(1)} %collective-permute-done.10.refs_3_), channel_id=1, source_target_pairs={{0,1},{1,0},{2,3},{3,2},{4,5},{5,4},{6,7},{7,6},{8,9},{9,8},{10,11... | collective-permute-start | bytes 3145736 | tf_op jit(solution)/shard_map/ppermute | solution.py:22
  128.9 28.2 %collective-permute-start.22 = (bf16[1152,512]{1,0:T(8,128)(2,1)}, bf16[1152,512]{1,0:T(8,128)(2,1)}, u32[]{:S(2)}, u32[]{:S(2)}) collective-permute-start(bf16[1152,512]{1,0:T(8,128)(2,1)} %collective-permute-done.8.refs_5_), channel_id=1, source_target_pairs={{8,0},{16,24},{9,1},{17,25},{10,2},{18,26},{11,3},{19,27},{12,4},{... | collective-permute-start | bytes 3538952 | tf_op jit(solution)/shard_map/ppermute | solution.py:199
  130.2 22.6 %collective-permute-start.25 = (bf16[512,1024]{1,0:T(8,128)(2,1)}, bf16[512,1024]{1,0:T(8,128)(2,1)}, u32[]{:S(2)}, u32[]{:S(2)}) collective-permute-start(bf16[512,1024]{1,0:T(8,128)(2,1)} %collective-permute-done.19.refs_9_), channel_id=1, source_target_pairs={{0,2},{2,0},{1,3},{3,1},{4,6},{6,4},{5,7},{7,5},{8,10},{10,8},{9,1... | collective-permute-start | bytes 3145736 | tf_op jit(solution)/shard_map/ppermute | solution.py:22
  131.1 43.1 %collective-permute-start.21 = (bf16[2,512,640]{2,1,0:T(8,128)(2,1)}, bf16[2,512,640]{2,1,0:T(8,128)(2,1)}, u32[]{:S(2)}, u32[]{:S(2)}) collective-permute-start(bf16[2,512,640]{2,1,0:T(8,128)(2,1)} %pad_maximum_fusion.2.refs_16_), channel_id=1, source_target_pairs={{0,8},{24,16},{1,9},{25,17},{2,10},{26,18},{3,11},{27,19},{4,12},{... | collective-permute-start | bytes 3932168 | tf_op jit(solution)/shard_map/ppermute | solution.py:199
  138.9 35.3 %collective-permute-start.23 = (bf16[1280,512]{1,0:T(8,128)(2,1)}, bf16[1280,512]{1,0:T(8,128)(2,1)}, u32[]{:S(2)}, u32[]{:S(2)}) collective-permute-start(bf16[1280,512]{1,0:T(8,128)(2,1)} %constant_dynamic-update-slice_fusion), channel_id=1, source_target_pairs={{8,16},{16,8},{9,17},{17,9},{10,18},{18,10},{11,19},{19,11},{12,20... | collective-permute-start | bytes 3932168 | tf_op jit(solution)/shard_map/ppermute | solution.py:199
  141.6 32.6 %collective-permute-start.24 = (bf16[2,512,640]{2,1,0:T(8,128)(2,1)}, bf16[2,512,640]{2,1,0:T(8,128)(2,1)}, u32[]{:S(2)}, u32[]{:S(2)}) collective-permute-start(bf16[2,512,640]{2,1,0:T(8,128)(2,1)} %pad_maximum_fusion.3), channel_id=1, source_target_pairs={{0,4},{4,0},{1,5},{5,1},{2,6},{6,2},{3,7},{7,3},{8,12},{12,8},{9,1... | collective-permute-start | bytes 3932168 | tf_op jit(solution)/shard_map/ppermute | solution.py:22
  152.8 25.5 %collective-permute-start.26 = (bf16[512,1024]{1,0:T(8,128)(2,1)}, bf16[512,1024]{1,0:T(8,128)(2,1)S(1)}, u32[]{:S(2)}, u32[]{:S(2)}) collective-permute-start(bf16[512,1024]{1,0:T(8,128)(2,1)} %copy-done.10), channel_id=1, source_target_pairs={{0,1},{1,0},{2,3},{3,2},{4,5},{5,4},{6,7},{7,6},{8,9},{9,8},{10,11... | collective-permute-start | bytes 3145736 | tf_op jit(solution)/shard_map/ppermute | solution.py:22
  157.0 24.0 %collective-permute-start.27 = (bf16[512,1024]{1,0:T(8,128)(2,1)}, bf16[512,1024]{1,0:T(8,128)(2,1)S(1)}, u32[]{:S(2)}, u32[]{:S(2)}) collective-permute-start(bf16[512,1024]{1,0:T(8,128)(2,1)} %collective-permute-done.18.refs_7_), channel_id=1, source_target_pairs={{0,1},{1,0},{2,3},{3,2},{4,5},{5,4},{6,7},{7,6},{8,9},{9,8},{10,11... | collective-permute-start | bytes 3145736 | tf_op jit(solution)/shard_map/ppermute | solution.py:22
  174.2 10.2 %collective-permute-start.28 = (bf16[512,1024]{1,0:T(8,128)(2,1)}, bf16[512,1024]{1,0:T(8,128)(2,1)}, u32[]{:S(2)}, u32[]{:S(2)}) collective-permute-start(bf16[512,1024]{1,0:T(8,128)(2,1)} %collective-permute-done.19.refs_9_), channel_id=1, source_target_pairs={{0,1},{1,0},{2,3},{3,2},{4,5},{5,4},{6,7},{7,6},{8,9},{9,8},{10,11... | collective-permute-start | bytes 3145736 | tf_op jit(solution)/shard_map/ppermute | solution.py:22
  174.8 11.3 %collective-permute-start.29 = (bf16[512,1024]{1,0:T(8,128)(2,1)}, bf16[512,1024]{1,0:T(8,128)(2,1)}, u32[]{:S(2)}, u32[]{:S(2)}) collective-permute-start(bf16[512,1024]{1,0:T(8,128)(2,1)} %collective-permute-done.25.refs_11_), channel_id=1, source_target_pairs={{0,1},{1,0},{2,3},{3,2},{4,5},{5,4},{6,7},{7,6},{8,9},{9,8},{10,11... | collective-permute-start | bytes 3145736 | tf_op jit(solution)/shard_map/ppermute | solution.py:22
  174.9 37.0 %collective-permute-start.30 = (bf16[2,512,640]{2,1,0:T(8,128)(2,1)}, bf16[2,512,640]{2,1,0:T(8,128)(2,1)}, u32[]{:S(2)}, u32[]{:S(2)}) collective-permute-start(bf16[2,512,640]{2,1,0:T(8,128)(2,1)} %collective-permute-done.24.refs_17_), channel_id=1, source_target_pairs={{0,8},{24,16},{1,9},{25,17},{2,10},{26,18},{3,11},{27,19},{4,12},{... | collective-permute-start | bytes 3932168 | tf_op jit(solution)/shard_map/ppermute | solution.py:199
  179.2 32.7 %collective-permute-start.32 = (bf16[1280,512]{1,0:T(8,128)(2,1)}, bf16[1280,512]{1,0:T(8,128)(2,1)}, u32[]{:S(2)}, u32[]{:S(2)}) collective-permute-start(bf16[1280,512]{1,0:T(8,128)(2,1)} %collective-permute-done.15.refs_15_.refs_16_), channel_id=1, source_target_pairs={{8,16},{16,8},{9,17},{17,9},{10,18},{18,10},{11,19},{19,11},{12,20... | collective-permute-start | bytes 3932168 | tf_op jit(solution)/shard_map/ppermute | solution.py:199
  182.0 29.9 %collective-permute-start.31 = (bf16[1152,512]{1,0:T(8,128)(2,1)}, bf16[1152,512]{1,0:T(8,128)(2,1)}, u32[]{:S(2)}, u32[]{:S(2)}) collective-permute-start(bf16[1152,512]{1,0:T(8,128)(2,1)} %collective-permute-done.17.refs_7_), channel_id=1, source_target_pairs={{8,0},{16,24},{9,1},{17,25},{10,2},{18,26},{11,3},{19,27},{12,4},{... | collective-permute-start | bytes 3538952 | tf_op jit(solution)/shard_map/ppermute | solution.py:199
  184.4 36.8 %collective-permute-start.33 = (bf16[512,1152]{1,0:T(8,128)(2,1)}, bf16[512,1152]{1,0:T(8,128)(2,1)}, u32[]{:S(2)}, u32[]{:S(2)}) collective-permute-start(bf16[512,1152]{1,0:T(8,128)(2,1)} %slice_bitcast_fusion), channel_id=1, source_target_pairs={{0,4},{4,0},{1,5},{5,1},{2,6},{6,2},{3,7},{7,3},{8,12},{12,8},{9,1... | collective-permute-start | bytes 3538952 | tf_op jit(solution)/shard_map/ppermute | solution.py:22
  (49 other events, 722.9 us)
